TPU v7x, 32 devices: a whole 2x2x4 slice. The times are simulated.
32 devices in a mesh: dp: 8 (over y, x, core), tensor: 4 (over z).
Axes of the slice: x: 2, y: 2, z: 4, core: 2. Of those that a mesh axis runs over, the one named last changes fastest.
Arguments:
- hidden_in: bfloat16 [8, 1024, 2048], P('dp', 'tensor'), may hold values from -6 to 6
- out_grad: bfloat16 [8, 1024, 2048], P('dp', 'tensor'), may hold values from -6 to 6
- doc_ids: int32 [8, 1024], P('dp'), may hold values from 0 to 1023, as said below
- expert_ids: int32 [8, 1024, 8], P('dp'), may hold values from 0 to 63, all different within a row; in each aligned block of 1024 rows (0 to 1023, 1024 to 2047, ..., all dimensions but the last counted through in order) at most 192 rows name the same one
- prenorm: bfloat16 [2048], P(('dp', 'tensor')), may hold values from 0.099609375 to 1.8984375
- querynorm: bfloat16 [128, 16], P('dp', 'tensor'), may hold values from 0.099609375 to 1.8984375
- keynorm: bfloat16 [128, 16], P('dp', 'tensor'), may hold values from 0.099609375 to 1.8984375
- query_proj: bfloat16 [2048, 2048], P('dp', 'tensor'), may hold values from -0.125 to 0.125
- key_proj: bfloat16 [2048, 2048], P('dp', 'tensor'), may hold values from -0.125 to 0.125
- value_proj: bfloat16 [2048, 2048], P('dp', 'tensor'), may hold values from -0.125 to 0.125
- output_proj: bfloat16 [2048, 2048], P('dp', 'tensor'), may hold values from -1.5 to 1.5
- postnorm: bfloat16 [2048], P(('dp', 'tensor')), may hold values from 0.099609375 to 1.8984375
- router: bfloat16 [2048, 64], P(('dp', 'tensor')), may hold values from -0.0625 to 0.0625
- gate_proj: bfloat16 [64, 2048, 1024], P('dp', None, 'tensor'), may hold values from -0.125 to 0.125
- up_proj: bfloat16 [64, 2048, 1024], P('dp', None, 'tensor'), may hold values from -0.125 to 0.125
- down_proj: bfloat16 [64, 2048, 1024], P('dp', None, 'tensor'), may hold values from -6 to 6
Outputs:
- layer_out: bfloat16 [8, 1024, 2048], P('dp', 'tensor')
- input_grad: bfloat16 [8, 1024, 2048], P('dp', 'tensor')
- prenorm_grad: float32 [2048], P(('dp', 'tensor'))
- querynorm_grad: float32 [128, 16], P('dp', 'tensor')
- keynorm_grad: float32 [128, 16], P('dp', 'tensor')
- query_grad: float32 [2048, 2048], P('dp', 'tensor')
- key_grad: float32 [2048, 2048], P('dp', 'tensor')
- value_grad: float32 [2048, 2048], P('dp', 'tensor')
- output_grad: float32 [2048, 2048], P('dp', 'tensor')
- postnorm_grad: float32 [2048], P(('dp', 'tensor'))
- router_grad: float32 [2048, 64], P(('dp', 'tensor'))
- gate_grad: float32 [64, 2048, 1024], P('dp', None, 'tensor')
- up_grad: float32 [64, 2048, 1024], P('dp', None, 'tensor')
- down_grad: float32 [64, 2048, 1024], P('dp', None, 'tensor')
Inputs may be any that keep to these rules, and one draw needn't show every extreme that they name: `expert_ids`: each row names 8 different experts; of the 1024 rows of one sequence at most 192 name any one expert. `doc_ids`: ids never fall along a sequence; the last token of every sequence has id 1024 - 1.
All inputs are finite; a program needn't handle non-finite values.
Results may differ from a plain program's by a relative error of at most 0.02.
Values may be sent and summed in bfloat16 or wider, within the bound.
A program may use at most 704 MiB of HBM per device.

v0:
```python
import functools

import jax
import jax.numpy as jnp
from jax import lax
from jax.experimental import pallas as pl
from jax.experimental.pallas import tpu as pltpu
from jax.sharding import PartitionSpec as P

D = 2048
HD = 128
E = 64
TOP = 8
CG = 192


epsilon = 1e-05
masked_score = -1000000000.0


def rope_tables(length, width):
    positions = jnp.arange(length).astype(jnp.float32)
    rates = 10000.0 ** (-jnp.arange(0, width, 2).astype(jnp.float32) / width)
    angles = positions[:, None] * rates[None, :]
    return (jnp.concatenate([jnp.cos(angles)] * 2, -1), jnp.concatenate([jnp.sin(angles)] * 2, -1))


def rotate(tensor):
    half = tensor.shape[-1] // 2
    return jnp.concatenate([-tensor[..., half:], tensor[..., :half]], -1)


def rotate_back(tensor):
    half = tensor.shape[-1] // 2
    return jnp.concatenate([tensor[..., half:], -tensor[..., :half]], -1)


def sum_heads(parts):
    return lax.psum((parts[0], parts[1]), "tensor")


def norm_back(grad, value, inverse, gain, width):
    scaled = grad * gain
    inner = jnp.sum(scaled * value, -1, keepdims=True)
    return inverse * scaled - value * inverse**3 * inner / width


def block_scores(query, keys, documents, start, block, scale):
    row_place = start + jnp.arange(block)
    col_place = jnp.arange(documents.shape[0])
    allowed = (documents[:, None] == documents[None, :]) & (
        row_place[:, None] >= col_place[None, :]
    )
    scores = jnp.einsum("qhd,khd->hqk", query, keys, preferred_element_type=jnp.float32) * scale
    return (jnp.where(allowed[None], scores, masked_score), query)


def attend_forward(query, keys, values, documents, block, scale):
    count = query.shape[0] // block

    def one(index):
        scores, rows = block_scores(query, keys, documents, index * block, block, scale)
        peak = jnp.max(scores, -1, keepdims=True)
        weights = jnp.exp(scores - peak)
        total = jnp.sum(weights, -1, keepdims=True)
        portion = (weights / total).astype(jnp.bfloat16)
        mixed = jnp.einsum("hqk,khd->qhd", portion, values, preferred_element_type=jnp.float32)
        return (mixed.astype(jnp.bfloat16), peak + jnp.log(total))

    mixed, logsum = lax.map(one, jnp.arange(count))
    return (mixed.reshape(query.shape), logsum)


def attend_backward(query, keys, values, documents, logsum, grad_mixed, block, scale):
    count = query.shape[0] // block

    def one(index):
        start = index * block
        scores, rows = block_scores(query, keys, documents, start, block, scale)
        portion = jnp.exp(scores - logsum[index])
        grad_portion = jnp.einsum(
            "qhd,khd->hqk", grad_mixed, values, preferred_element_type=jnp.float32
        )
        center = jnp.sum(portion * grad_portion, -1, keepdims=True)
        grad_scores = (portion * (grad_portion - center)).astype(jnp.bfloat16)
        grad_values = jnp.einsum(
            "hqk,qhd->khd",
            portion.astype(jnp.bfloat16),
            grad_mixed,
            preferred_element_type=jnp.float32,
        )
        grad_query = (
            jnp.einsum("hqk,khd->qhd", grad_scores, keys, preferred_element_type=jnp.float32)
            * scale
        )
        grad_keys = (
            jnp.einsum("hqk,qhd->khd", grad_scores, rows, preferred_element_type=jnp.float32)
            * scale
        )
        return (grad_query, grad_keys, grad_values)

    grad_query, grad_keys, grad_values = lax.map(one, jnp.arange(count))
    return (grad_query.reshape(query.shape), jnp.sum(grad_keys, 0), jnp.sum(grad_values, 0))


MESH = pl.DeviceIdType.MESH
VMEM = 60 * 1024 * 1024


def transfer(microseconds):
    return pl.CostEstimate(flops=0, bytes_accessed=microseconds * 3_000_000, transcendentals=0)


def flip(index, bit):
    return index + bit - 2 * bit * ((index // bit) % 2)


def send(source, target, send_sem, recv_sem, device):
    return pltpu.make_async_remote_copy(
        src_ref=source,
        dst_ref=target,
        send_sem=send_sem,
        recv_sem=recv_sem,
        device_id=device,
        device_id_type=MESH,
    )


def greet(devices, extra=()):
    barrier = pltpu.get_barrier_semaphore()
    for device in devices:
        pl.semaphore_signal(barrier, inc=1, device_id=device, device_id_type=MESH)
    for there, device in extra:

        @pl.when(there)
        def _(device=device):
            pl.semaphore_signal(barrier, inc=1, device_id=device, device_id_type=MESH)

    count = len(devices)
    for there, _ in extra:
        count = count + jnp.where(there, 1, 0)
    pl.semaphore_wait(barrier, count)


def both_ways(n):
    spot = lax.axis_index("tensor")
    return spot, (
        (spot < n - 1, {"tensor": jnp.minimum(spot + 1, n - 1)}),
        (spot > 0, {"tensor": jnp.maximum(spot - 1, 0)}),
    )


def shard_at(spot, way, distance, n):
    number = spot - distance if way == 0 else spot + distance
    return (number >= 0) & (number < n), jnp.clip(number, 0, n - 1)


def chain_gather_kernel(n, pieces, passing, own, *refs):
    refs = refs[passing:]
    if len(refs) > passing + 4:
        small, out, everything, *sems = refs[0], refs[1], refs[2 + passing], *refs[3 + passing :]
        local_sem, send_sem, recv_sem, all_send, all_recv = sems
        finish = spread_start(n, small, everything, all_send, all_recv)
    else:
        out, (local_sem, send_sem, recv_sem) = refs[0], refs[1 + passing :]
        finish = None
    spot, sides = both_ways(n)
    rows = own.shape[0] // pieces
    if finish is None:
        greet([], sides)
    keep = pltpu.make_async_copy(own, out.at[spot], local_sem)
    keep.start()

    def copy(way, distance, piece):
        there, number = shard_at(spot, way, distance, n)
        part = pl.ds(piece * rows, rows)
        source = own.at[part] if distance == 0 else out.at[number, part]
        return there & sides[way][0], send(
            source,
            out.at[number, part],
            send_sem.at[way, distance, piece],
            recv_sem.at[way, distance, piece],
            sides[way][1],
        )

    def arrived(way, distance, piece):
        there, number = shard_at(spot, way, distance, n)
        part = pl.ds(piece * rows, rows)

        @pl.when(there)
        def _():
            send(
                out.at[number, part],
                out.at[number, part],
                send_sem.at[way, distance - 1, piece],
                recv_sem.at[way, distance - 1, piece],
                sides[way][1],
            ).wait_recv()

    for distance in range(n):
        for piece in range(pieces):
            for way in (0, 1):
                if distance:
                    arrived(way, distance, piece)
                if distance < n - 1:
                    go, one = copy(way, distance, piece)

                    @pl.when(go)
                    def _(one=one):
                        one.start()

    keep.wait()
    for distance in range(n - 1):
        for piece in range(pieces):
            for way in (0, 1):
                go, one = copy(way, distance, piece)

                @pl.when(go)
                def _(one=one):
                    one.wait_send()

    if finish is not None:
        finish()


def chain_gather(own, later, number, small=None, pieces=4):
    n = lax.axis_size("tensor")
    rows, width = own.shape
    anywhere = pl.BlockSpec(memory_space=pl.ANY)
    inside = pl.BlockSpec(memory_space=pltpu.VMEM)
    sem = pltpu.SemaphoreType.DMA
    outs = [jax.ShapeDtypeStruct((n, rows, width), own.dtype)]
    outs += [jax.ShapeDtypeStruct(one.shape, one.dtype) for one in later]
    more, sems = [], []
    if small is not None:
        count = lax.axis_size("dp") * n
        outs.append(jax.ShapeDtypeStruct((count,) + small.shape, small.dtype))
        more, sems = [small], [sem((count,)), sem((count,))]
    plain = [anywhere] * (1 + len(later)) + [inside] * len(more)
    out, *rest = pl.pallas_call(
        functools.partial(chain_gather_kernel, n, pieces, len(later)),
        out_shape=outs,
        in_specs=plain,
        out_specs=plain,
        input_output_aliases={1 + index: 1 + index for index in range(len(later))},
        scratch_shapes=[sem, sem((2, n - 1, pieces)), sem((2, n - 1, pieces))] + sems,
        compiler_params=pltpu.CompilerParams(
            collective_id=number, has_side_effects=True, vmem_limit_bytes=VMEM
        ),
        cost_estimate=transfer(65),
        name="chain_gather",
    )(own, *later, *more)
    return (out.reshape(n * rows, width), *rest)


def add_into(target, source, rows, start=0, source_start=0):
    step = 16

    def body(index, carry):
        at = pl.ds(pl.multiple_of(start + index * step, step), step)
        come = pl.ds(pl.multiple_of(source_start + index * step, step), step)
        target[at, :] = (
            target[at, :].astype(jnp.float32) + source[come, :].astype(jnp.float32)
        ).astype(target.dtype)
        return carry

    lax.fori_loop(0, rows // step, body, 0)


def chain_sum_kernel(n, pieces, part, _later, out, _passed, held, send_sem, recv_sem):
    spot, sides = both_ways(n)
    greet([], sides)
    onward, finish, drain = chain_steps(n, pieces, part, out, held, send_sem, recv_sem)
    for far in range(n - 1, 0, -1):
        onward(far)
    finish()
    drain()


def chain_steps(n, pieces, part, out, held, send_sem, recv_sem):
    spot, sides = both_ways(n)
    rows = out.shape[0] // pieces

    def copy(way, far, piece, mine):
        number = spot + far if way == 0 else spot - far
        there = (number >= 0) & (number < n)
        number = jnp.clip(number, 0, n - 1)
        at = pl.ds(piece * rows, rows)
        source = part.at[number, at]
        return there, number, send(
            source if mine else held.at[way, far, at],
            held.at[way, far - 1, at],
            send_sem.at[way, far - 1, piece],
            recv_sem.at[way, far - 1, piece],
            sides[way][1],
        )

    def arrived(way, far, piece):
        at = pl.ds(piece * rows, rows)
        send(
            held.at[way, far, at],
            held.at[way, far, at],
            send_sem.at[way, far, piece],
            recv_sem.at[way, far, piece],
            sides[way][1],
        ).wait_recv()

    def onward(far):
        for piece in range(pieces):
            for way in (0, 1):
                behind = sides[1 - way][0]
                there, number, first = copy(way, far, piece, True)

                @pl.when(there & jnp.logical_not(behind))
                def _(first=first):
                    first.start()

                if far < n - 1:
                    _, _, again = copy(way, far, piece, False)

                    @pl.when(there & behind)
                    def _(way=way, piece=piece, number=number, again=again):
                        arrived(way, far, piece)
                        add_into(
                            held.at[way, far], part.at[number], rows, piece * rows, piece * rows
                        )
                        again.start()

    def finish():
        for piece in range(pieces):

            def body(index, carry, piece=piece):
                here = pl.ds(pl.multiple_of(piece * rows + index * 16, 16), 16)
                out[here, :] = part[spot, here, :].astype(jnp.float32)
                return carry

            lax.fori_loop(0, rows // 16, body, 0)
            for way in (0, 1):

                @pl.when(sides[1 - way][0])
                def _(way=way, piece=piece):
                    arrived(way, 0, piece)
                    add_into(out, held.at[way, 0], rows, piece * rows, piece * rows)

    def drain():
        for far in range(n - 1, 0, -1):
            for piece in range(pieces):
                for way in (0, 1):
                    there, _, one = copy(way, far, piece, True)

                    @pl.when(there)
                    def _(one=one):
                        one.wait_send()

    return onward, finish, drain


def chain_sum(part, later, number, pieces=4):
    n = lax.axis_size("tensor")
    width = part.shape[1]
    rows = part.shape[0] // n
    anywhere = pl.BlockSpec(memory_space=pl.ANY)
    inside = pl.BlockSpec(memory_space=pltpu.VMEM)
    return pl.pallas_call(
        functools.partial(chain_sum_kernel, n, pieces),
        out_shape=[
            jax.ShapeDtypeStruct((rows, width), jnp.float32),
            jax.ShapeDtypeStruct(later.shape, later.dtype),
        ],
        in_specs=[inside, anywhere],
        out_specs=[inside, anywhere],
        input_output_aliases={1: 1},
        scratch_shapes=[
            pltpu.VMEM((2, n - 1, rows, width), part.dtype),
            pltpu.SemaphoreType.DMA((2, n - 1, pieces)),
            pltpu.SemaphoreType.DMA((2, n - 1, pieces)),
        ],
        compiler_params=pltpu.CompilerParams(
            collective_id=number, has_side_effects=True, vmem_limit_bytes=VMEM
        ),
        cost_estimate=transfer(65),
        name="chain_sum",
    )(part.reshape(n, rows, width), later)


def box_devices():
    me = lax.axis_index("dp")
    return me, {bit: {"dp": flip(me, bit)} for bit in (1, 2, 4)}


def box_gather_kernel(n, own, out, local_sem, z_send, z_recv, near_send, near_recv, on_send, on_recv, side_send, side_recv):
    spot, sides = both_ways(n)
    me, near = box_devices()
    half = own.shape[0] // 2
    greet([near[1], near[2], near[4]], sides)
    keep = pltpu.make_async_copy(own, out.at[me, spot], local_sem)
    keep.start()
    sends = []

    def piece(seq, shard, part):
        return out.at[seq, shard, pl.ds(part * half, half)]

    def start(condition, one):
        sends.append((condition, one))

        @pl.when(condition)
        def _():
            one.start()

    def await_piece(condition, target, recv):
        @pl.when(condition)
        def _():
            send(target, target, side_send.at[0, 0, 0], recv, near[1]).wait_recv()

    def to_side(condition, slot, seq, shard, part, source):
        start(condition, send(source, piece(seq, shard, part), side_send.at[slot, shard, part], side_recv.at[slot, shard, part], near[1]))

    def mine(way, distance):
        there, shard = shard_at(spot, way, distance, n)
        for part in (0, 1):
            if distance:
                await_piece(there, piece(me, shard, part), z_recv.at[way, distance - 1, part])
            source = piece(me, shard, part) if distance else own.at[pl.ds(part * half, half)]
            for out_way in (0, 1) if distance == 0 else (way,):
                if distance < n - 1:
                    start(there & sides[out_way][0], send(source, piece(me, shard, part), z_send.at[out_way, distance, part], z_recv.at[out_way, distance, part], sides[out_way][1]))
            for axis, bit in ((0, 2), (1, 4)):
                start(there, send(source, piece(me, shard, part), near_send.at[axis, shard, part], near_recv.at[axis, shard, part], near[bit]))
            to_side(there, 0, me, shard, part, source)

    def nearby(way, distance):
        there, shard = shard_at(spot, way, distance, n)
        for part in (0, 1):
            for axis, bit in ((0, 2), (1, 4)):
                seq = flip(me, bit)
                source = piece(seq, shard, part)
                await_piece(there, source, near_recv.at[axis, shard, part])
                if part == axis:
                    start(there, send(source, source, on_send.at[1 - axis, shard], on_recv.at[1 - axis, shard], near[6 - bit]))
                to_side(there, 1 + axis, seq, shard, part, source)

    def far(way, distance):
        there, shard = shard_at(spot, way, distance, n)
        seq = flip(flip(me, 2), 4)
        for part in (0, 1):
            source = piece(seq, shard, part)
            await_piece(there, source, on_recv.at[1 - part, shard])
            to_side(there, 3, seq, shard, part, source)

    for step in range(n + 2):
        for task, delay in ((mine, 0), (nearby, 1), (far, 2)):
            distance = step - delay
            if 0 <= distance < n:
                for way in (0, 1) if distance else (0,):
                    task(way, distance)
    for shard in range(n):
        for part in (0, 1):
            for slot, bit in enumerate((0, 2, 4, 6)):
                seq = flip(me, 1)
                for one in (2, 4):
                    if bit & one:
                        seq = flip(seq, one)
                await_piece(spot >= 0, piece(seq, shard, part), side_recv.at[slot, shard, part])
    keep.wait()
    for condition, one in sends:

        @pl.when(condition)
        def _(one=one):
            one.wait_send()


def box_gather(own):
    n = lax.axis_size("tensor")
    rows, width = own.shape
    sem = pltpu.SemaphoreType.DMA
    out = pl.pallas_call(
        functools.partial(box_gather_kernel, n),
        out_shape=jax.ShapeDtypeStruct((8, n, rows, width), own.dtype),
        in_specs=[pl.BlockSpec(memory_space=pl.ANY)],
        out_specs=pl.BlockSpec(memory_space=pl.ANY),
        scratch_shapes=[sem]
        + [sem((2, n - 1, 2))] * 2
        + [sem((2, n, 2))] * 2
        + [sem((2, n))] * 2
        + [sem((4, n, 2))] * 2,
        compiler_params=pltpu.CompilerParams(collective_id=3, has_side_effects=True),
        cost_estimate=transfer(75),
        name="box_gather",
    )(own)
    return out.reshape(8 * n * rows, width)


def order_of(spot, n):
    table = [sorted(range(n), key=lambda s: -abs(s - j)) for j in range(n)]
    result = []
    for step in range(n):
        value = jnp.int32(table[0][step])
        for j in range(1, n):
            value = jnp.where(spot == j, table[j][step], value)
        result.append(value)
    return result


def box_steps(n, pieces, part_at, final, side, local, on, near, chain, local_sem, side_send, side_recv, on_send, on_recv, near_send, near_recv, z_send, z_recv):
    spot, sides = both_ways(n)
    me, close = box_devices()
    rows = side.shape[2]
    half = rows // 2
    bits = (6, 2, 4, 0)
    sends = []

    def seq_of(index, bit):
        for one in (2, 4):
            if bit & one:
                index = flip(index, one)
        return index

    def start(one, condition=None):
        sends.append((condition, one))
        if condition is None:
            one.start()
        else:

            @pl.when(condition)
            def _():
                one.start()

    def await_at(target, recv):
        send(target, target, side_send.at[0, 0], recv, close[1]).wait_recv()

    def loads(chip, shard):
        return pltpu.make_async_copy(
            part_at(seq_of(me, bits[chip]), shard), local.at[chip, shard], local_sem.at[chip, shard]
        )

    def merge(chip, shard):
        await_at(side.at[chip, shard], side_recv.at[chip, shard])
        loads(chip, shard).wait()
        add_into(side.at[chip, shard], local.at[chip, shard], rows)

    def begin():
        for shard, _ in pieces:
            for chip in range(4):
                start(
                    send(
                        part_at(seq_of(flip(me, 1), bits[chip]), shard),
                        side.at[chip, shard],
                        side_send.at[chip, shard],
                        side_recv.at[chip, shard],
                        close[1],
                    )
                )
                loads(chip, shard).start()

    def first(step):
        shard = pieces[step][0]
        merge(0, shard)
        for axis, bit in ((0, 2), (1, 4)):
            start(
                send(
                    side.at[0, shard, pl.ds(axis * half, half)],
                    on.at[axis, shard],
                    on_send.at[axis, shard],
                    on_recv.at[axis, shard],
                    close[bit],
                )
            )
        merge(1, shard)
        merge(2, shard)

    def second(step):
        shard = pieces[step][0]
        for axis, bit in ((0, 2), (1, 4)):
            other = 2 - axis
            await_at(on.at[axis, shard], on_recv.at[axis, shard])
            add_into(side.at[other, shard], on.at[axis, shard], half, axis * half, 0)
            start(
                send(
                    side.at[other, shard],
                    near.at[1 - axis, shard],
                    near_send.at[1 - axis, shard],
                    near_recv.at[1 - axis, shard],
                    close[6 - bit],
                )
            )
        merge(3, shard)

    def third(step):
        shard = pieces[step][0]
        for axis in (0, 1):
            await_at(near.at[axis, shard], near_recv.at[axis, shard])
            add_into(side.at[3, shard], near.at[axis, shard], rows)

    def fourth(step):
        shard, kind = pieces[step]
        if kind == "far":
            for way in (0, 1):
                ahead = shard > spot if way == 0 else shard < spot
                distance = jnp.clip(shard - spot if way == 0 else spot - shard, 1, n - 1)

                @pl.when(ahead & sides[1 - way][0])
                def _(way=way, distance=distance):
                    slot = jnp.minimum(distance, n - 2)
                    await_at(chain.at[way, slot], z_recv.at[way, slot])
                    add_into(side.at[3, shard], chain.at[way, slot], rows)

                start(
                    send(
                        side.at[3, shard],
                        chain.at[way, distance - 1],
                        z_send.at[way, distance - 1],
                        z_recv.at[way, distance - 1],
                        sides[way][1],
                    ),
                    ahead,
                )
            return
        out = final(step)

        def body(index, carry):
            at = pl.ds(pl.multiple_of(index * 16, 16), 16)
            out[at, :] = side[3, shard, at, :].astype(jnp.float32)
            return carry

        lax.fori_loop(0, rows // 16, body, 0)
        if kind == "own":
            for way in (0, 1):

                @pl.when(sides[1 - way][0])
                def _(way=way):
                    await_at(chain.at[way, 0], z_recv.at[way, 0])
                    add_into(out, chain.at[way, 0], rows)

    def drain():
        for condition, one in sends:
            if condition is None:
                one.wait_send()
            else:

                @pl.when(condition)
                def _(one=one):
                    one.wait_send()

    return begin, first, second, third, fourth, drain


def greet_box(n):
    _, sides = both_ways(n)
    _, close = box_devices()
    greet([close[1], close[2], close[4]], sides)


def box_scratch(n, pieces, rows, width, kind):
    sem = pltpu.SemaphoreType.DMA
    return [
        pltpu.VMEM((4, pieces, rows, width), kind),
        pltpu.VMEM((4, pieces, rows, width), kind),
        pltpu.VMEM((2, pieces, rows // 2, width), kind),
        pltpu.VMEM((2, pieces, rows, width), kind),
        pltpu.VMEM((2, n - 1, rows, width), kind),
        sem((4, pieces)),
        sem((4, pieces)),
        sem((4, pieces)),
        sem((2, pieces)),
        sem((2, pieces)),
        sem((2, pieces)),
        sem((2, pieces)),
        sem((2, n - 1)),
        sem((2, n - 1)),
    ]


def box_sum_kernel(n, passing, part, tokens, *refs):
    out, token_out = refs[passing : passing + 2]
    held, send_sem, recv_sem, *scratch = refs[2 * passing + 2 :]
    onward, finish, end = chain_steps(n, 4, tokens, token_out, held, send_sem, recv_sem)
    spot, _ = both_ways(n)
    greet_box(n)
    order = order_of(spot, n)
    pieces = [(shard, "far") for shard in order[:-1]] + [(order[-1], "own")]
    begin, *tasks, drain = box_steps(
        n, pieces, lambda seq, shard: part.at[seq, shard], lambda step: out, *scratch
    )
    begin()
    for step in range(n + 3):
        if step < n - 1:
            onward(n - 1 - step)
        for delay, task in enumerate(tasks):
            if 0 <= step - delay < n:
                task(step - delay)
    finish()
    end()
    drain()


def closing_kernel(n, tokens, part, _later, out, weights, _passed, *scratch):
    spot, _ = both_ways(n)
    greet_box(n)
    held, send_sem, recv_sem = scratch[:3]
    onward, finish, end = chain_steps(n, 4, tokens, out, held, send_sem, recv_sem)
    order = order_of(spot, n)
    flat = weights.shape[0] - 1
    pieces = [(shard, "far") for shard in order[:-1]]
    pieces += [(n + index, "flat") for index in range(flat)] + [(order[-1], "own")]
    targets = [None] * (n - 1) + [weights.at[1 + index] for index in range(flat)] + [weights.at[0]]
    begin, first, second, third, fourth, drain = box_steps(
        n, pieces, lambda seq, shard: part.at[shard, seq], lambda step: targets[step], *scratch[3:]
    )
    begin()
    onward(n - 1)
    count = len(pieces)
    far = n - 2
    for task in (first, second, third, fourth):
        for step in range(count):
            task(step)
        if far:
            onward(far)
            far -= 1
    for left in range(far, 0, -1):
        onward(left)
    finish()
    end()
    drain()


def closing(tokens, part, later):
    n = lax.axis_size("tensor")
    pieces, _, rows, width = part.shape
    sem = pltpu.SemaphoreType.DMA
    inside = pl.BlockSpec(memory_space=pltpu.VMEM)
    anywhere = pl.BlockSpec(memory_space=pl.ANY)
    return pl.pallas_call(
        functools.partial(closing_kernel, n),
        out_shape=[
            jax.ShapeDtypeStruct(tokens.shape[1:], jnp.float32),
            jax.ShapeDtypeStruct((pieces - n + 1, rows, width), jnp.float32),
            jax.ShapeDtypeStruct(later.shape, later.dtype),
        ],
        in_specs=[inside, anywhere, anywhere],
        out_specs=[inside, inside, anywhere],
        input_output_aliases={2: 2},
        scratch_shapes=[
            pltpu.VMEM((2, n - 1) + tokens.shape[1:], tokens.dtype),
            sem((2, n - 1, 4)),
            sem((2, n - 1, 4)),
        ]
        + box_scratch(n, pieces, rows, width, part.dtype),
        compiler_params=pltpu.CompilerParams(
            collective_id=8, has_side_effects=True, vmem_limit_bytes=VMEM
        ),
        cost_estimate=transfer(80),
        name="closing",
    )(tokens, part, later)


def swap_kernel(n, part, _later, out, _passed, local_sem, send_sem, recv_sem):
    spot = lax.axis_index("tensor")
    greet([{"tensor": lax.rem(spot + step, n)} for step in range(1, n)])
    keep = pltpu.make_async_copy(part.at[spot], out.at[spot], local_sem)
    keep.start()

    def copy(step):
        to = lax.rem(spot + step, n)
        return send(
            part.at[to], out.at[spot], send_sem.at[step], recv_sem.at[step], {"tensor": to}
        )

    for step in range(1, n):
        copy(step).start()
    keep.wait()
    for step in range(1, n):
        come = lax.rem(spot - step + n, n)
        send(
            part.at[come], out.at[come], send_sem.at[step], recv_sem.at[step], {"tensor": come}
        ).wait_recv()
        copy(step).wait_send()


def swap(part, later, number):
    n = lax.axis_size("tensor")
    sem = pltpu.SemaphoreType.DMA
    anywhere = pl.BlockSpec(memory_space=pl.ANY)
    return pl.pallas_call(
        functools.partial(swap_kernel, n),
        out_shape=[
            jax.ShapeDtypeStruct(part.shape, part.dtype),
            jax.ShapeDtypeStruct(later.shape, later.dtype),
        ],
        in_specs=[anywhere] * 2,
        out_specs=[anywhere] * 2,
        input_output_aliases={1: 1},
        scratch_shapes=[sem, sem((n,)), sem((n,))],
        compiler_params=pltpu.CompilerParams(
            collective_id=number, has_side_effects=True, vmem_limit_bytes=VMEM
        ),
        cost_estimate=transfer(25),
        name="swap",
    )(part, later)


def box_sum(part, tokens, later):
    n = lax.axis_size("tensor")
    width = part.shape[1]
    rows = part.shape[0] // (8 * n)
    kind = part.dtype
    anywhere = pl.BlockSpec(memory_space=pl.ANY)
    inside = pl.BlockSpec(memory_space=pltpu.VMEM)
    tokens = tokens.reshape(n, -1, width)
    sem = pltpu.SemaphoreType.DMA
    out, token_out, *later = pl.pallas_call(
        functools.partial(box_sum_kernel, n, len(later)),
        out_shape=[
            jax.ShapeDtypeStruct((rows, width), jnp.float32),
            jax.ShapeDtypeStruct(tokens.shape[1:], jnp.float32),
        ]
        + [jax.ShapeDtypeStruct(one.shape, one.dtype) for one in later],
        in_specs=[anywhere, inside] + [anywhere] * len(later),
        out_specs=[inside] * 2 + [anywhere] * len(later),
        input_output_aliases={2 + index: 2 + index for index in range(len(later))},
        scratch_shapes=[
            pltpu.VMEM((2, n - 1) + tokens.shape[1:], tokens.dtype),
            sem((2, n - 1, 4)),
            sem((2, n - 1, 4)),
        ]
        + box_scratch(n, n, rows, width, kind),
        compiler_params=pltpu.CompilerParams(
            collective_id=4, has_side_effects=True, vmem_limit_bytes=VMEM
        ),
        cost_estimate=transfer(90),
        name="box_sum",
    )(part.reshape(8, n, rows, width), tokens, *later)
    return out, token_out, later


def everyone(n):
    count = lax.axis_size("dp") * n
    me = lax.axis_index("dp") * n + lax.axis_index("tensor")

    def device(number):
        return {"dp": number // n, "tensor": number % n}

    return count, me, device


def greet_all(count, me, device):
    barrier = pltpu.get_barrier_semaphore()

    def signal(step, carry):
        pl.semaphore_signal(barrier, inc=1, device_id=device(lax.rem(me + step, count)), device_id_type=MESH)
        return carry

    lax.fori_loop(1, count, signal, 0)
    pl.semaphore_wait(barrier, count - 1)


def spread_start(n, own, out, send_sem, recv_sem):
    count, me, device = everyone(n)
    greet_all(count, me, device)
    out[me] = own[...]

    def copy(step):
        to = device(lax.rem(me + step, count))
        return send(own, out.at[me], send_sem.at[step], recv_sem.at[step], to)

    def go(step, carry):
        copy(step).start()
        return carry

    def end(step, carry):
        copy(step).wait_send()
        come = lax.rem(me - step + count, count)
        send(own, out.at[come], send_sem.at[step], recv_sem.at[step], device(come)).wait_recv()
        return carry

    lax.fori_loop(1, count, go, 0)
    return lambda: lax.fori_loop(1, count, end, 0)


def sum_spread_kernel(n, part, out, held, send_sem, recv_sem):
    count, me, device = everyone(n)
    greet_all(count, me, device)
    out[...] = part[me]

    def copy(step):
        to = lax.rem(me + step, count)
        return send(part.at[to], held.at[me], send_sem.at[step], recv_sem.at[step], device(to))

    def go(step, carry):
        copy(step).start()
        return carry

    def end(step, carry):
        come = lax.rem(me - step + count, count)
        send(part.at[0], held.at[come], send_sem.at[step], recv_sem.at[step], device(come)).wait_recv()
        out[...] += held[come]
        copy(step).wait_send()
        return carry

    lax.fori_loop(1, count, go, 0)
    lax.fori_loop(1, count, end, 0)


def sum_spread(part):
    n = lax.axis_size("tensor")
    count = lax.axis_size("dp") * n
    sem = pltpu.SemaphoreType.DMA
    return pl.pallas_call(
        functools.partial(sum_spread_kernel, n),
        out_shape=jax.ShapeDtypeStruct(part.shape[1:], part.dtype),
        in_specs=[pl.BlockSpec(memory_space=pltpu.VMEM)],
        out_specs=pl.BlockSpec(memory_space=pltpu.VMEM),
        scratch_shapes=[pltpu.VMEM(part.shape, part.dtype), sem((count,)), sem((count,))],
        compiler_params=pltpu.CompilerParams(
            collective_id=6, has_side_effects=True, vmem_limit_bytes=VMEM
        ),
        cost_estimate=transfer(20),
        name="sum_spread",
    )(part)


TB = 256
GR = 16
TILE = 256
EXTRA = 2 * E
def ceil_to(value, unit):
    return (value + unit - 1) // unit * unit


def nt_dot(a, b):
    return lax.dot_general(a, b, (((1,), (1,)), ((), ())), preferred_element_type=jnp.float32)


def tn_dot(a, b):
    return lax.dot_general(a, b, (((0,), (0,)), ((), ())), preferred_element_type=jnp.float32)


def nn_dot(a, b):
    return jnp.dot(a, b, preferred_element_type=jnp.float32)


def pair(value):
    high = value.astype(jnp.bfloat16)
    low = (value - high.astype(jnp.float32)).astype(jnp.bfloat16)
    return high, low


def unpair(value):
    value = value.astype(jnp.float32)
    return value[:, :E] + value[:, E:]


def excl_cumsum(value, axis):
    return jnp.cumsum(value, axis) - value


class Plan:
    def __init__(self, tokens, seq_len, local):
        seqs = tokens // seq_len
        self.tokens, self.local = tokens, local
        self.blocks = tokens // TB
        per_seq = seq_len // TB
        worst = min(CG + (GR - 1) * per_seq, seq_len)
        self.cap = ceil_to(seqs * worst // GR * GR, TILE)
        groups = (seqs * local * CG + self.blocks * local * (GR - 1)) // GR
        self.slots = ceil_to(TB * TOP * local // E + local * GR, 64)
        self.items = groups * GR // self.slots + self.blocks
        self.tiles = self.cap // TILE


def pick_at(here, table):
    return jnp.sum(jnp.where(here, table[None, :], 0), 1)


def steps_of(size, steps):
    first = excl_cumsum(steps, 0)
    used = jnp.sum(steps)
    index = jnp.minimum(jnp.arange(size), used - 1)
    owner = jnp.sum((first[None, :] <= index[:, None]).astype(jnp.int32), 1) - 1
    here = owner[:, None] == jnp.arange(steps.shape[0])[None, :]
    part = index - pick_at(here, first)
    last = (part == pick_at(here, steps) - 1).astype(jnp.int32)
    return first, used, owner, part, last, here


def routing(plan, routes, base):
    local, blocks = plan.local, plan.blocks
    mine = base + jnp.arange(local)
    picked = jnp.any(routes[:, :, None] == mine[None, None, :], 1)
    grid = picked.reshape(blocks, TB, local)
    ones = grid.astype(jnp.bfloat16)
    earlier = (jnp.arange(TB)[:, None] > jnp.arange(TB)[None, :]).astype(jnp.bfloat16)
    rank = jnp.einsum("ts,bse->bte", earlier, ones, preferred_element_type=jnp.float32).astype(
        jnp.int32
    )
    count = jnp.sum(grid.astype(jnp.int32), 1)
    groups = (count + GR - 1) // GR
    inner = excl_cumsum(groups, 1)
    total = jnp.sum(groups, 1)
    outer = excl_cumsum(groups, 0)
    expert_rows = jnp.sum(groups, 0) * GR
    place = jnp.where(grid, inner[:, None, :] * GR + rank, -1)
    items = jnp.maximum((total * GR + plan.slots - 1) // plan.slots, 1)
    first, used, block, part, last, here = steps_of(plan.items, items)
    wide, slots = plan.slots // GR, plan.cap // GR
    spot = jnp.arange(slots)[None, :, None]
    low = outer.T[:, None, :]
    inside = (spot >= low) & (spot < low + groups.T[:, None, :])
    origin = first[None, :] * wide + inner.T
    source = jnp.sum(jnp.where(inside, origin[:, None, :] + spot - low, 0), 2)
    tiles = jnp.maximum((expert_rows + TILE - 1) // TILE, 1)
    _, tiles_used, owner, tile, tile_last, _ = steps_of(local * plan.tiles, tiles)

    def at_block(table):
        return jnp.sum(jnp.where(here[:, :, None], table[None], 0), 1)[:, None, :]

    spot = (part[:, None] * wide + jnp.arange(wide)[None, :])[:, :, None]
    low, many, begin = at_block(inner), at_block(groups), at_block(outer)
    inside = (spot >= low) & (spot < low + many)
    target = jnp.sum(
        jnp.where(inside, (jnp.arange(local) * slots)[None, None, :] + begin + spot - low, 0), 2
    )
    return dict(
        place=place,
        used=used[None],
        block=block,
        part=part,
        last=last,
        source=source.reshape(-1),
        filled=expert_rows,
        tiles_used=tiles_used[None],
        owner=owner,
        tile=tile,
        tile_last=tile_last,
        target=target.reshape(-1),
    )


def while_used(step, used, *refs):
    @pl.when(pl.program_id(0) < used[0])
    def _():
        step(used, *refs)


def dispatch_step(used, block, part, post, grad, router, place, *refs):
    rows, share, held = refs[len(refs) // 2 - 1], refs[len(refs) // 2], refs[-1]
    step = pl.program_id(0)
    local = place.shape[1]
    slots = rows.shape[0]

    @pl.when(part[step] == 0)
    def _():
        portion = jax.nn.softmax(nn_dot(post[...], router[...]), -1)
        high, low = pair(portion)
        both = jnp.concatenate([high, low], 1)
        held[...] = both
        share[...] = both

    slot = lax.broadcasted_iota(jnp.int32, (slots, TB), 0) + part[step] * slots
    hit = slot == place[0, 0:1, :]
    for one in range(1, local):
        hit = hit | (slot == place[0, one : one + 1, :])
    pick = jnp.where(hit, 1.0, 0.0).astype(jnp.bfloat16)
    rows[:, :D] = nn_dot(pick, post[...]).astype(jnp.bfloat16)
    rows[:, D : 2 * D] = nn_dot(pick, grad[...]).astype(jnp.bfloat16)
    rows[:, 2 * D :] = nn_dot(pick, held[...]).astype(jnp.bfloat16)


def dispatch(plan, route, post, grad, router, later):
    wide = 2 * D + EXTRA
    place = route["place"].transpose(0, 2, 1)

    def at_block(step, used, block, part):
        return (block[step], 0)

    return pl.pallas_call(
        functools.partial(while_used, dispatch_step),
        grid_spec=pltpu.PrefetchScalarGridSpec(
            num_scalar_prefetch=3,
            grid=(plan.items,),
            in_specs=[
                pl.BlockSpec((TB, D), at_block),
                pl.BlockSpec((TB, D), at_block),
                pl.BlockSpec((D, E), lambda step, used, block, part: (0, 0)),
                pl.BlockSpec((1, plan.local, TB), lambda step, used, block, part: (block[step], 0, 0)),
            ]
            + [pl.BlockSpec(memory_space=pl.ANY)] * len(later),
            out_specs=[
                pl.BlockSpec((plan.slots, wide), lambda step, used, block, part: (jnp.minimum(step, used[0] - 1), 0)),
                pl.BlockSpec((TB, EXTRA), at_block),
            ]
            + [pl.BlockSpec(memory_space=pl.ANY)] * len(later),
            scratch_shapes=[pltpu.VMEM((TB, EXTRA), jnp.bfloat16)],
        ),
        out_shape=[
            jax.ShapeDtypeStruct((plan.items * plan.slots, wide), jnp.bfloat16),
            jax.ShapeDtypeStruct((plan.tokens, EXTRA), jnp.bfloat16),
        ]
        + [jax.ShapeDtypeStruct(one.shape, one.dtype) for one in later],
        input_output_aliases={7 + index: 2 + index for index in range(len(later))},
        compiler_params=pltpu.CompilerParams(vmem_limit_bytes=VMEM),
        cost_estimate=transfer(45),
        name="dispatch",
    )(route["used"], route["block"], route["part"], post, grad, router, place, *later)


def fetch_groups(table, rows, held, sems, step, count):
    slot = lax.rem(step, 2)
    for index in range(count):
        group = table[step * count + index]
        pltpu.make_async_copy(
            rows.at[pl.ds(pl.multiple_of(group * GR, GR), GR)],
            held.at[slot, pl.ds(index * GR, GR)],
            sems.at[slot],
        ).start()


def await_groups(rows, held, sems, step, count):
    slot = lax.rem(step, 2)
    pltpu.make_async_copy(rows.at[pl.ds(0, count * GR)], held.at[slot], sems.at[slot]).wait()


def next_groups(used, table, rows, held, sems, count):
    step = pl.program_id(0)

    @pl.when(step == 0)
    def _():
        fetch_groups(table, rows, held, sems, step, count)

    @pl.when(step + 1 < used[0])
    def _():
        fetch_groups(table, rows, held, sems, step + 1, count)

    await_groups(rows, held, sems, step, count)
    return lax.rem(step, 2)


def expert_step(
    used, source, owner, tile, last, filled, base, all_rows, w_gate, w_up, w_down, *refs
):
    *before, result, gate_out, up_out, down_out, held, sems, gate_sum, up_sum, down_sum = refs
    step = pl.program_id(0)
    count = TILE // GR
    slot = next_groups(used, source, all_rows, held, sems, count)
    expert, part = owner[step], tile[step]

    @pl.when(part == 0)
    def _():
        gate_sum[...] = jnp.zeros_like(gate_sum)
        up_sum[...] = jnp.zeros_like(up_sum)
        down_sum[...] = jnp.zeros_like(down_sum)

    @pl.when(last[step] == 1)
    def _():
        def clear(index, carry):
            at = pl.ds(pl.multiple_of(index * GR, GR), GR)
            held[slot, at, :] = jnp.zeros((GR, held.shape[2]), held.dtype)
            return carry

        lax.fori_loop((filled[expert] - part * TILE) // GR, count, clear, 0)

    number = base[0] + expert
    rows, upstream = held[slot, :, :D], held[slot, :, D : 2 * D]
    shares = held[slot, :, 2 * D :]
    lane = lax.broadcasted_iota(jnp.int32, (TILE, EXTRA), 1)
    own = (lane == number) | (lane == number + E)
    gate = jnp.sum(jnp.where(own, shares.astype(jnp.float32), 0.0), -1, keepdims=True)
    gate_pre = nn_dot(rows, w_gate[0])
    up_pre = nn_dot(rows, w_up[0])
    plain = nn_dot(upstream, w_down[0])
    squash = jax.nn.sigmoid(gate_pre)
    swish = gate_pre * squash
    active = (swish * up_pre).astype(jnp.bfloat16).astype(jnp.float32)
    change = jnp.sum(active * plain, -1, keepdims=True)
    grad_active = gate * plain
    grad_gate = (grad_active * up_pre * squash * (1.0 + gate_pre * (1.0 - squash))).astype(
        jnp.bfloat16
    )
    grad_up = (grad_active * swish).astype(jnp.bfloat16)
    scaled = (gate * active).astype(jnp.bfloat16)
    result[:, :D] = nt_dot(scaled, w_down[0]).astype(jnp.bfloat16)
    result[:, D : 2 * D] = (nt_dot(grad_gate, w_gate[0]) + nt_dot(grad_up, w_up[0])).astype(
        jnp.bfloat16
    )
    high, low = pair(change)
    result[:, 2 * D :] = jnp.where(
        lane == number,
        high.astype(jnp.float32),
        jnp.where(lane == number + E, low.astype(jnp.float32), 0.0),
    ).astype(jnp.bfloat16)
    gate_sum[...] += tn_dot(grad_gate, rows)
    up_sum[...] += tn_dot(grad_up, rows)
    down_sum[...] += tn_dot(scaled, upstream)

    @pl.when(last[step] == 1)
    def _():
        for index, (out, total) in enumerate(
            ((gate_out, gate_sum), (up_out, up_sum), (down_out, down_sum))
        ):
            out[0] = total[...].T + before[index][0] if before else total[...].T


def experts(plan, route, base, rows, w_gate, w_up, w_down, before):
    wide = 2 * D + EXTRA
    width = w_gate.shape[2]
    slots, count = plan.cap // GR, TILE // GR
    table = route["source"].reshape(plan.local * plan.tiles, count)
    number = route["owner"] * (slots // count) + route["tile"]
    table = table[number].reshape(-1)

    def whole(step, used, table, owner, tile, last, filled, base):
        return (owner[step], 0, 0)

    def tile_at(step, used, table, owner, tile, last, filled, base):
        return (owner[step] * plan.tiles + tile[step], 0)

    weight = pl.BlockSpec((1, D, width), whole)
    total = plan.local * plan.cap
    return pl.pallas_call(
        functools.partial(while_used, expert_step),
        grid_spec=pltpu.PrefetchScalarGridSpec(
            num_scalar_prefetch=7,
            grid=(plan.local * plan.tiles,),
            in_specs=[pl.BlockSpec(memory_space=pl.ANY)] + [weight] * (3 + len(before)),
            out_specs=[pl.BlockSpec((TILE, wide), tile_at)] + [weight] * 3,
            scratch_shapes=[
                pltpu.VMEM((2, TILE, wide), jnp.bfloat16),
                pltpu.SemaphoreType.DMA((2,)),
            ]
            + [pltpu.VMEM((width, D), jnp.float32)] * 3,
        ),
        out_shape=[jax.ShapeDtypeStruct((total, wide), jnp.bfloat16)]
        + [jax.ShapeDtypeStruct((plan.local, D, width), jnp.float32)] * 3,
        compiler_params=pltpu.CompilerParams(vmem_limit_bytes=VMEM),
        input_output_aliases={11 + index: 1 + index for index in range(len(before))},
        cost_estimate=transfer(80),
        name="experts",
    )(
        route["tiles_used"],
        table,
        route["owner"],
        route["tile"],
        route["tile_last"],
        route["filled"],
        base[None],
        rows,
        w_gate,
        w_up,
        w_down,
        *before,
    )


def combine_step(
    used, target, block, part, last, results, place, share, post, router, *refs
):
    held, sems, sums = refs[-3:]
    passing = (len(refs) - 6) // 2
    out, grad, router_out = refs[passing : passing + 3]
    step = pl.program_id(0)
    local = place.shape[1]
    slots = held.shape[1]

    at = next_groups(used, target, results, held, sems, slots // GR)

    @pl.when(step == 0)
    def _():
        router_out[...] = jnp.zeros_like(router_out)

    slot = lax.broadcasted_iota(jnp.int32, (TB, slots), 1) + part[step] * slots
    hit = slot == place[:, 0:1]
    for one in range(1, local):
        hit = hit | (slot == place[:, one : one + 1])
    pick = jnp.where(hit, 1.0, 0.0).astype(jnp.bfloat16)

    def term(begin, end):
        return nn_dot(pick, held[at, :, begin:end])

    def finish(value):
        change = unpair(value(2 * D, 2 * D + EXTRA))
        portion = unpair(share[...])
        moved = portion * (change - jnp.sum(change * portion, -1, keepdims=True))
        moved = moved.astype(jnp.bfloat16)
        out[...] = value(0, D).astype(jnp.bfloat16)
        grad[...] = (value(D, 2 * D) + nt_dot(moved, router[...])).astype(jnp.bfloat16)
        router_out[...] += tn_dot(moved, post[...])

    single = (part[step] == 0) & (last[step] == 1)

    @pl.when(single)
    def _():
        finish(term)

    @pl.when(jnp.logical_not(single))
    def _():
        @pl.when(part[step] == 0)
        def _():
            sums[...] = jnp.zeros_like(sums)

        sums[...] += term(0, 2 * D + EXTRA)

        @pl.when(last[step] == 1)
        def _():
            finish(lambda begin, end: sums[:, begin:end])


def combine(plan, route, results, share, post, router, later):
    wide = 2 * D + EXTRA

    def at_block(step, used, target, block, part, last):
        return (block[step], 0)

    def fixed(step, used, target, block, part, last):
        return (0, 0)

    return pl.pallas_call(
        functools.partial(while_used, combine_step),
        grid_spec=pltpu.PrefetchScalarGridSpec(
            num_scalar_prefetch=5,
            grid=(plan.items,),
            in_specs=[
                pl.BlockSpec(memory_space=pl.ANY),
                pl.BlockSpec((TB, plan.local), at_block),
                pl.BlockSpec((TB, EXTRA), at_block),
                pl.BlockSpec((TB, D), at_block),
                pl.BlockSpec((D, E), fixed),
            ]
            + [pl.BlockSpec(memory_space=pl.ANY)] * len(later),
            out_specs=[
                pl.BlockSpec((TB, D), at_block),
                pl.BlockSpec((TB, D), at_block),
                pl.BlockSpec((E, D), fixed),
            ]
            + [pl.BlockSpec(memory_space=pl.ANY)] * len(later),
            scratch_shapes=[
                pltpu.VMEM((2, plan.slots, wide), jnp.bfloat16),
                pltpu.SemaphoreType.DMA((2,)),
                pltpu.VMEM((TB, wide), jnp.float32),
            ],
        ),
        out_shape=[
            jax.ShapeDtypeStruct((plan.tokens, D), jnp.bfloat16),
            jax.ShapeDtypeStruct((plan.tokens, D), jnp.bfloat16),
            jax.ShapeDtypeStruct((E, D), jnp.float32),
        ]
        + [jax.ShapeDtypeStruct(one.shape, one.dtype) for one in later],
        input_output_aliases={10 + index: 3 + index for index in range(len(later))},
        compiler_params=pltpu.CompilerParams(vmem_limit_bytes=VMEM),
        cost_estimate=transfer(50),
        name="combine",
    )(
        route["used"],
        route["target"],
        route["block"],
        route["part"],
        route["last"],
        results,
        route["place"].reshape(plan.tokens, plan.local),
        share,
        post,
        router,
        *later,
    )


def gather_all(own):
    if lax.axis_size("dp") == 8:
        return box_gather(own)
    return lax.all_gather(
        lax.all_gather(own, "tensor", axis=0, tiled=True), "dp", axis=0, tiled=True
    )


def gather_slowly(own):
    if lax.axis_size("dp") == 8:
        return lax.all_gather(own, ("dp", "tensor"), axis=0, tiled=True)
    return gather_all(own)


def gather_output(own):
    n = lax.axis_size("tensor")
    if lax.axis_size("dp") == 8:
        everything = lax.all_gather(own, ("dp", "tensor"), axis=0, tiled=False)
        everything = everything.reshape((8, n) + own.shape).transpose(1, 0, 2, 3)
        return everything.reshape(n, -1, own.shape[1])
    part = lax.all_gather(own, "dp", axis=0, tiled=True)
    return lax.all_gather(part, "tensor", axis=0, tiled=False)


def sum_last(tokens, parts, later):
    n = lax.axis_size("tensor")
    if lax.axis_size("dp") == 8:
        return closing(
            tokens.reshape(n, -1, tokens.shape[1]),
            parts.reshape(parts.shape[0], 8, -1, parts.shape[2]),
            later,
        )
    tokens, later = chain_sum(tokens, later, 8)
    parts = lax.psum_scatter(parts, "dp", scatter_dimension=1, tiled=True)
    own = lax.psum_scatter(parts[:n], "tensor", scatter_dimension=0, tiled=True)
    return tokens, jnp.concatenate([own, parts[n:]]).astype(jnp.float32), later


def sum_all(part, tokens, later):
    if lax.axis_size("dp") == 8:
        return box_sum(part, tokens, later)
    tokens = lax.psum_scatter(tokens, "tensor", scatter_dimension=0, tiled=True)
    return sum_slowly(part).astype(jnp.float32), tokens.astype(jnp.float32), later


def sum_slowly(part):
    part = lax.psum_scatter(part, "dp", scatter_dimension=0, tiled=True)
    return lax.psum_scatter(part, "tensor", scatter_dimension=0, tiled=True)


def fill(value, rows, columns):
    return jnp.pad(value, ((0, rows - value.shape[0]), (0, columns - value.shape[1])))


def pack_small(router, prenorm, postnorm, querynorm, keynorm, routes):
    n = lax.axis_size("tensor")
    rank = lax.axis_index("tensor")
    rows = router.shape[0]
    head = ceil_to(max(rows, querynorm.shape[0]), 16)
    heads = querynorm.shape[1]
    block = jnp.concatenate(
        [
            fill(router, head, E),
            fill(prenorm[:, None], head, 1),
            fill(postnorm[:, None], head, 1),
            fill(querynorm, head, heads),
            fill(keynorm, head, heads),
        ],
        1,
    )
    part = routes.shape[0] // n
    own = lax.dynamic_slice_in_dim(routes, rank * part, part, 0)
    own = own.astype(jnp.bfloat16).reshape(-1, 128)
    tail = ceil_to(own.shape[0], 16)
    return jnp.concatenate([fill(block, head, 128), fill(own, tail, 128)], 0)


def unpack_small(everything, router, querynorm, routes):
    n = lax.axis_size("tensor")
    rank = lax.axis_index("tensor")
    rows, heads = router.shape[0], querynorm.shape[1]
    head = ceil_to(max(rows, querynorm.shape[0]), 16)
    part = routes.size // n // 128
    total = everything.shape[1]
    mine = everything.reshape(-1, n, total, 128)[:, rank]
    at = E + 2
    return (
        everything[:, :rows, :E].reshape(-1, E),
        everything[:, :rows, E].reshape(-1).astype(jnp.float32),
        everything[:, :rows, E + 1].reshape(-1).astype(jnp.float32),
        mine[:, : querynorm.shape[0], at : at + heads].reshape(-1, heads),
        mine[:, : querynorm.shape[0], at + heads : at + 2 * heads].reshape(-1, heads),
        everything[:, head : head + part].reshape(-1, TOP).astype(jnp.int32),
    )


def body(
    hidden_in,
    out_grad,
    doc_ids,
    expert_ids,
    prenorm,
    querynorm,
    keynorm,
    query_proj,
    key_proj,
    value_proj,
    output_proj,
    postnorm,
    router,
    gate_proj,
    up_proj,
    down_proj,
):
    residual = hidden_in[0].astype(jnp.float32)
    upstream = out_grad[0]
    documents = doc_ids[0]
    routes = expert_ids[0]
    shard = residual.shape[0]
    seq_len = documents.shape[0]
    mesh_dp = lax.axis_size("dp")
    block = min(seq_len, 1024)
    scale = HD ** (-0.5)
    cosine, sine = rope_tables(seq_len, HD)
    small = pack_small(router, prenorm, postnorm, querynorm, keynorm, routes)
    group_hidden, later, output_late, everything = chain_gather(
        hidden_in[0], [upstream[: shard // 2], output_proj], 1, small
    )
    router_full, pre_gain, post_gain, gain_query, gain_key, all_routes = unpack_small(
        everything, router, querynorm, routes
    )
    weights = lax.all_gather(
        jnp.concatenate([query_proj, key_proj, value_proj], 1),
        "dp",
        axis=0,
        tiled=True,
    )
    w_query, w_key, w_value = jnp.split(weights, 3, 1)
    w_output = gather_output(output_late)
    heads = w_query.shape[1] // HD
    query_scale = gain_query.astype(jnp.float32).T.reshape(-1)
    key_scale = gain_key.astype(jnp.float32).T.reshape(-1)
    inv_pre = lax.rsqrt(jnp.mean(residual * residual, -1, keepdims=True) + epsilon)
    group_hidden = group_hidden.astype(jnp.float32)
    group_inv = lax.rsqrt(jnp.mean(group_hidden * group_hidden, -1, keepdims=True) + epsilon)
    group_normed = (group_hidden * group_inv * pre_gain).astype(jnp.bfloat16)
    n = lax.axis_size("tensor")
    few = shard // 2
    plan = Plan(mesh_dp * n * few, n * few, gate_proj.shape[0])
    base = (lax.axis_index("dp") * plan.local).astype(jnp.int32)
    all_routes = all_routes.reshape(mesh_dp, n, 2, few, TOP)
    route = [
        routing(plan, all_routes[:, :, index].reshape(-1, TOP), base) for index in range(2)
    ]
    all_grad = [gather_slowly(later)]
    query = jnp.dot(group_normed, w_query, preferred_element_type=jnp.float32)
    keys = jnp.dot(group_normed, w_key, preferred_element_type=jnp.float32)
    values = jnp.dot(group_normed, w_value, preferred_element_type=jnp.float32).astype(jnp.bfloat16)
    query_sq, key_sq = sum_heads(
        (jnp.sum(query * query, -1, keepdims=True), jnp.sum(keys * keys, -1, keepdims=True))
    )
    inv_query = lax.rsqrt(query_sq / D + epsilon)
    inv_key = lax.rsqrt(key_sq / D + epsilon)
    query_heads = (query * inv_query * query_scale).reshape(seq_len, heads, HD)
    key_heads = (keys * inv_key * key_scale).reshape(seq_len, heads, HD)
    query_rot = (query_heads * cosine[:, None] + rotate(query_heads) * sine[:, None]).astype(
        jnp.bfloat16
    )
    key_rot = (key_heads * cosine[:, None] + rotate(key_heads) * sine[:, None]).astype(jnp.bfloat16)
    value_heads = values.reshape(seq_len, heads, HD)
    mixed, logsum = attend_forward(query_rot, key_rot, value_heads, documents, block, scale)
    mixed_flat = mixed.reshape(seq_len, heads * HD)
    mixed_own, later = swap(mixed_flat.reshape(n, shard, heads * HD), upstream[few:], 7)
    all_grad.append(gather_slowly(later))
    attn_local = sum(nt_dot(mixed_own[index], w_output[index]) for index in range(n))
    middle = residual + attn_local
    inv_post = lax.rsqrt(jnp.mean(middle * middle, -1, keepdims=True) + epsilon)
    post_normed = (middle * inv_post * post_gain).astype(jnp.bfloat16)
    all_post = [gather_all(post_normed[:few]), gather_slowly(post_normed[few:])]
    grads, outs, backs, router_parts = [], [], [], []
    for index in range(2):
        rows, portion, *outs = dispatch(
            plan, route[index], all_post[index], all_grad[index], router_full, outs
        )
        results, *grads = experts(
            plan, route[index], base, rows, gate_proj, up_proj, down_proj, grads
        )
        if index == 0:
            later = [all_post[1], all_grad[1]]
        else:
            later = [lax.psum_scatter(backs[0], "dp", scatter_dimension=0, tiled=True)]
        out, back, router_part, *later = combine(
            plan, route[index], results, portion, all_post[index], router_full, later
        )
        if index == 0:
            all_post[1], all_grad[1] = later
        else:
            early = later[0]
        outs.append(out)
        backs.append(back)
        router_parts.append(router_part)
    gate_weight_grad, up_weight_grad, down_weight_grad = grads
    first_out = lax.psum_scatter(outs[0], "dp", scatter_dimension=0, tiled=True)
    early = jnp.concatenate(
        [early.reshape(n, few, D), first_out.reshape(n, few, D)], 1
    ).reshape(-1, D)
    late, early, outs = sum_all(backs[1], early, outs[1:])
    early, first_out = early[:few], early[few:].astype(jnp.bfloat16)
    grad_post = jnp.concatenate([early, late], 0)
    moe_local = jnp.concatenate([first_out, sum_slowly(outs[0])], 0)
    router_part = router_parts[0] + router_parts[1]
    router_part = router_part.T
    post_gain_part = jnp.sum(grad_post * middle * inv_post, 0)
    grad_middle = upstream.astype(jnp.float32) + norm_back(
        grad_post, middle, inv_post, post_gain, D
    )
    change = grad_middle.astype(jnp.bfloat16)
    grad_mixed, _ = swap(
        jnp.stack([nn_dot(change, w_output[index]).astype(jnp.bfloat16) for index in range(n)]),
        jnp.zeros((16, 128), jnp.bfloat16),
        2,
    )
    output_parts = [tn_dot(change, mixed_own[index]).astype(jnp.bfloat16) for index in range(n)]
    grad_query_rot, grad_key_rot, grad_value_heads = attend_backward(
        query_rot,
        key_rot,
        value_heads,
        documents,
        logsum,
        grad_mixed.reshape(seq_len, heads, HD),
        block,
        scale,
    )
    grad_query_flat = (
        grad_query_rot * cosine[:, None] + rotate_back(grad_query_rot * sine[:, None])
    ).reshape(seq_len, -1)
    grad_key_flat = (
        grad_key_rot * cosine[:, None] + rotate_back(grad_key_rot * sine[:, None])
    ).reshape(seq_len, -1)
    query_inner, key_inner = sum_heads(
        (
            jnp.sum(grad_query_flat * query_scale * query, -1, keepdims=True),
            jnp.sum(grad_key_flat * key_scale * keys, -1, keepdims=True),
        )
    )
    grad_query = (
        inv_query * query_scale * grad_query_flat - query * inv_query**3 * query_inner / D
    ).astype(jnp.bfloat16)
    grad_key = (inv_key * key_scale * grad_key_flat - keys * inv_key**3 * key_inner / D).astype(
        jnp.bfloat16
    )
    query_gain_part = jnp.sum(grad_query_flat * query * inv_query, 0).reshape(heads, HD).T
    key_gain_part = jnp.sum(grad_key_flat * keys * inv_key, 0).reshape(heads, HD).T
    grad_value = grad_value_heads.reshape(seq_len, -1).astype(jnp.bfloat16)
    query_part = lax.dot_general(
        group_normed, grad_query, (((0,), (0,)), ((), ())), preferred_element_type=jnp.float32
    )
    key_part = lax.dot_general(
        group_normed, grad_key, (((0,), (0,)), ((), ())), preferred_element_type=jnp.float32
    )
    value_part = lax.dot_general(
        group_normed, grad_value, (((0,), (0,)), ((), ())), preferred_element_type=jnp.float32
    )
    normed_term = lax.dot_general(
        grad_query, w_query, (((1,), (1,)), ((), ())), preferred_element_type=jnp.float32
    )
    normed_term = normed_term + lax.dot_general(
        grad_key, w_key, (((1,), (1,)), ((), ())), preferred_element_type=jnp.float32
    )
    normed_term = normed_term + lax.dot_general(
        grad_value, w_value, (((1,), (1,)), ((), ())), preferred_element_type=jnp.float32
    )
    grad_normed, weight_sums, middle = sum_last(
        normed_term.astype(jnp.bfloat16),
        jnp.stack(
            output_parts + [part.astype(jnp.bfloat16) for part in (query_part, key_part, value_part)]
        ),
        middle,
    )
    layer_out = (middle + moe_local.astype(jnp.float32)).astype(jnp.bfloat16)[None]
    pre_gain_part = jnp.sum(grad_normed * residual * inv_pre, 0)
    input_grad = (grad_middle + norm_back(grad_normed, residual, inv_pre, pre_gain, D)).astype(
        jnp.bfloat16
    )[None]
    gains = jnp.concatenate([query_gain_part, key_gain_part], 1).reshape(mesh_dp, 1, -1, 2 * heads)
    mine = jnp.arange(n)[None, :, None, None] == lax.axis_index("tensor")
    gains = jnp.pad(
        jnp.where(mine, gains, 0.0),
        ((0, 0), (0, 0), (0, max(router.shape[0] - HD // mesh_dp, 0)), (0, 0)),
    ).reshape(D, 2 * heads)
    small = jnp.concatenate(
        [
            router_part,
            pre_gain_part[:, None],
            post_gain_part[:, None],
            gains,
            jnp.zeros((D, 128 - E - 2 - 2 * heads), jnp.float32),
        ],
        1,
    )
    small = sum_spread(small.reshape(-1, router.shape[0], 128))
    gain_grads = small[: HD // mesh_dp, E + 2 : E + 2 + 2 * heads]
    return (
        layer_out,
        input_grad,
        small[:, E],
        gain_grads[:, :heads],
        gain_grads[:, heads : 2 * heads],
        weight_sums[1],
        weight_sums[2],
        weight_sums[3],
        weight_sums[0],
        small[:, E + 1],
        small[:, :E],
        gate_weight_grad,
        up_weight_grad,
        down_weight_grad,
    )


def solution(mesh):
    in_specs = (
        P("dp", "tensor", None),
        P("dp", "tensor", None),
        P("dp", None),
        P("dp", None, None),
        P(("dp", "tensor")),
        P("dp", "tensor"),
        P("dp", "tensor"),
        P("dp", "tensor"),
        P("dp", "tensor"),
        P("dp", "tensor"),
        P("dp", "tensor"),
        P(("dp", "tensor")),
        P(("dp", "tensor"), None),
        P("dp", None, "tensor"),
        P("dp", None, "tensor"),
        P("dp", None, "tensor"),
    )
    out_specs = (
        P("dp", "tensor", None),
        P("dp", "tensor", None),
        P(("dp", "tensor")),
        P("dp", "tensor"),
        P("dp", "tensor"),
        P("dp", "tensor"),
        P("dp", "tensor"),
        P("dp", "tensor"),
        P("dp", "tensor"),
        P(("dp", "tensor")),
        P(("dp", "tensor"), None),
        P("dp", None, "tensor"),
        P("dp", None, "tensor"),
        P("dp", None, "tensor"),
    )
    return jax.shard_map(body, mesh=mesh, in_specs=in_specs, out_specs=out_specs, check_vma=False)
```

profile of v0, /device:TPU:0, one launch (start us, length us, event | category | flops | bytes accessed | tf_op | source)
XLA Modules:
  0.0 1315.6 jit_solution(4137424141413457383)
XLA Ops:
  14.4 89.4 %chain_gather.1 = (bf16[4,256,2048]{2,1,0:T(8,128)(2,1)}, bf16[128,2048]{1,0:T(8,128)(2,1)}, bf16[256,512]{1,0:T(8,128)(2,1)}, bf16[32,80,128]{2,1,0:T(8,128)(2,1)}) custom-call(bf16[256,2048]{1,0:T(8,128)(2,1)} %bitcast.353, bf16[128,2048]{1,0:T(8,128)(2,1)} %get-tuple-element.282.refs_0_, ...), custom_call_target="tpu_custom_call", output_to_operand_aliasing={{1}: (1, {}), {2}: (2, {})} | custom-call | bytes 195000000 | tf_op jit(solution)/shard_map/chain_gather/pallas_call | solution.py:240
  127.2 10.6 all-reduce.5
  149.0 7.8 fusion.136
  156.8 8.1 fusion
  164.9 7.8 fusion.52
  175.3 22.5 %swap.2 = (bf16[4,256,512]{2,1,0:T(8,128)(2,1)}, bf16[128,2048]{1,0:T(8,128)(2,1)}) custom-call(bf16[4,256,512]{2,1,0:T(8,128)(2,1)} %copy.180.part, bf16[128,2048]{1,0:T(8,128)(2,1)} %get-tuple-element.281._later), custom_call_target="tpu_custom_call", output_to_operand_aliasing={{1}: (1, {})} | custom-call | bytes 75000000 | tf_op jit(solution)/shard_map/swap/pallas_call | solution.py:783
  236.8 112.9 %box_gather.1 = bf16[8,4,128,2048]{3,2,1,0:T(8,128)(2,1)} custom-call(bf16[128,2048]{1,0:T(8,128)(2,1)} %get-tuple-element.280.own), custom_call_target="tpu_custom_call" | custom-call | bytes 225000000 | tf_op jit(solution)/shard_map/box_gather/pallas_call | solution.py:476
  349.8 46.2 %dispatch.2 = (bf16[20352,4224]{1,0:T(8,128)(2,1)}, bf16[4096,128]{1,0:T(8,128)(2,1)}) custom-call(s32[1]{0:T(128)} %bitcast.52.used, s32[53]{0:T(128)} %copy-done.90, s32[53]{0:T(128)} %copy-done.92, bf16[4096,2048]{1,0:T(8,128)(2,1)} %bitcast.351, bf16[4096,2048]{1,0:T(8,128)(2,1)} %all-gather.9.cloned.1.call-done.refs_3_, bf16[2048,64]{1,0:T(8,128)(2,1)} %bitcast.360, ...), custom_call_target="tpu_custom_call" | custom-call | bytes 135000000 | tf_op jit(solution)/shard_map/dispatch/pallas_call | solution.py:1075
  396.0 95.3 %experts.2 = (bf16[14336,4224]{1,0:T(8,128)(2,1)}, f32[8,2048,256]{2,1,0:T(8,128)}, f32[8,2048,256]{2,1,0:T(8,128)}, f32[8,2048,256]{2,1,0:T(8,128)}) custom-call(s32[1]{0:T(128)} %bitcast.55.used, s32[896]{0:T(1024)} %reshape.1102.refs_0_, s32[56]{0:T(128)} %copy-done.97, s32[56]{0:T(128)} %get-tuple-element.238.refs_2_, s32[56]{0:T(128)} %get-tuple-element.237.refs_3_, ...), custom_call_target="tpu_custom_call" | custom-call | bytes 240000000 | tf_op jit(solution)/shard_map/experts/pallas_call | solution.py:1218
  491.4 74.6 %all-gather.11.cloned.1.call-done.refs_9_ = bf16[4096,2048]{1,0:T(8,128)(2,1)} async-done(((bf16[128,2048]{1,0:T(8,128)(2,1)}), bf16[4096,2048]{1,0:T(8,128)(2,1)}) %all-gather.11.cloned.1.call-update) | async-done | bytes 16777232 | tf_op jit(solution)/shard_map/all_gather | solution.py:1375
  565.9 53.3 %combine.2 = (bf16[4096,2048]{1,0:T(8,128)(2,1)}, bf16[4096,2048]{1,0:T(8,128)(2,1)}, f32[64,2048]{1,0:T(8,128)}, bf16[4096,2048]{1,0:T(8,128)(2,1)}, bf16[4096,2048]{1,0:T(8,128)(2,1)}) custom-call(s32[1]{0:T(128)} %bitcast.52.used, s32[1272]{0:T(1024)} %reshape.1100.refs_0_, s32[53]{0:T(128)} %copy-done.90, ...), custom_call_target="tpu_custom_call", output_to_operand_aliasing={{3}: (10, {}), {4}: (11, {})} | custom-call | bytes 150000000 | tf_op jit(solution)/shard_map/combine/pallas_call | solution.py:1315
  620.9 47.5 %dispatch.3 = (bf16[20352,4224]{1,0:T(8,128)(2,1)}, bf16[4096,128]{1,0:T(8,128)(2,1)}, bf16[4096,2048]{1,0:T(8,128)(2,1)}) custom-call(s32[1]{0:T(128)} %bitcast.37.used, s32[53]{0:T(128)} %copy-done.89, s32[53]{0:T(128)} %get-tuple-element.257.refs_1_.refs_2_, ...), custom_call_target="tpu_custom_call", output_to_operand_aliasing={{2}: (7, {})} | custom-call | bytes 135000000 | tf_op jit(solution)/shard_map/dispatch/pallas_call | solution.py:1075
  674.6 110.5 %experts.3 = (bf16[14336,4224]{1,0:T(8,128)(2,1)}, f32[8,2048,256]{2,1,0:T(8,128)}, f32[8,2048,256]{2,1,0:T(8,128)}, f32[8,2048,256]{2,1,0:T(8,128)}) custom-call(s32[1]{0:T(128)} %bitcast.40.used, s32[896]{0:T(1024)} %reshape.1097.refs_0_, s32[56]{0:T(128)} %copy-done.96, ...), custom_call_target="tpu_custom_call", output_to_operand_aliasing={{1}: (11, {}), {2}: (12, {}), {3}: (13, {})} | custom-call | bytes 240000000 | tf_op jit(solution)/shard_map/experts/pallas_call | solution.py:1218
  785.2 54.8 %combine.3 = (bf16[4096,2048]{1,0:T(8,128)(2,1)}, bf16[4096,2048]{1,0:T(8,128)(2,1)}, f32[64,2048]{1,0:T(8,128)}, bf16[512,2048]{1,0:T(8,128)(2,1)}) custom-call(s32[1]{0:T(128)} %bitcast.37.used, s32[1272]{0:T(1024)} %reshape.1095.refs_0_, s32[53]{0:T(128)} %copy-done.89, s32[53]{0:T(128)} %get-tuple-element.257.refs_1_.refs_2_, ...), custom_call_target="tpu_custom_call", output_to_operand_aliasing={{3}: (10, {})} | custom-call | bytes 150000000 | tf_op jit(solution)/shard_map/combine/pallas_call | solution.py:1315
  840.0 16.6 %reduce-scatter.7.cloned.1.call-done = bf16[512,2048]{1,0:T(8,128)(2,1)} async-done(((bf16[4096,2048]{1,0:T(8,128)(2,1)}), bf16[512,2048]{1,0:T(8,128)(2,1)}) %reduce-scatter.7.cloned.1.call-update) | async-done | bytes 2097168 | tf_op jit(solution)/shard_map/reduce_scatter | solution.py:1567
  861.4 105.3 %box_sum.1 = (f32[128,2048]{1,0:T(8,128)}, f32[256,2048]{1,0:T(8,128)}, bf16[4096,2048]{1,0:T(8,128)(2,1)}) custom-call(bf16[8,4,128,2048]{3,2,1,0:T(8,128)(2,1)} %bitcast.358, bf16[4,256,2048]{2,1,0:T(8,128)(2,1)} %pad_maximum_fusion.tokens, bf16[4096,2048]{1,0:T(8,128)(2,1)} %get-tuple-element.122.refs_0_), custom_call_target="tpu_custom_call", output_to_operand_aliasing={{2}: (2, {})} | custom-call | bytes 270000000 | tf_op jit(solution)/shard_map/box_sum/pallas_call | solution.py:810
  992.7 38.3 %swap.3 = (bf16[4,256,512]{2,1,0:T(8,128)(2,1)}, bf16[16,128]{1,0:T(8,128)(2,1)}) custom-call(bf16[4,256,512]{2,1,0:T(8,128)(2,1)} %pad_maximum_fusion.2.part, bf16[16,128]{1,0:T(8,128)(2,1)} %broadcast_in_dim.380._later), custom_call_target="tpu_custom_call", output_to_operand_aliasing={{1}: (1, {})} | custom-call | bytes 75000000 | tf_op jit(solution)/shard_map/swap/pallas_call | solution.py:783
  1035.8 11.0 multiply_reduce_fusion
  1046.8 8.3 multiply_convert_fusion
  1058.6 6.4 bitcast_multiply_fusion.4
  1072.3 16.5 %all-reduce.4 = (f32[1024]{0:T(1024)S(1)}, f32[1024]{0:T(1024)}) all-reduce(f32[1024]{0:T(1024)S(1)} %get-tuple-element.192, f32[1024]{0:T(1024)S(1)} %get-tuple-element.194), channel_id=1, replica_groups=mesh['dp'=8,'tensor'=4] {'tensor'}, use_global_device_ids=true, to_apply=%region_55.56 | all-reduce | flops 2048 | bytes 16384 | tf_op jit(solution)/shard_map/psum | solution.py:39
  1118.3 6.2 convolution_convert_fusion
  1144.4 111.1 %closing.1 = (f32[256,2048]{1,0:T(8,128)}, f32[4,256,512]{2,1,0:T(8,128)}, f32[256,2048]{1,0:T(8,128)}) custom-call(bf16[4,256,2048]{2,1,0:T(8,128)(2,1)} %bitcast.359, bf16[7,8,256,512]{3,2,1,0:T(8,128)(2,1)} %constant_dynamic-update-slice_fusion.part, f32[256,2048]{1,0:T(8,128)} %copy-done.1), custom_call_target="tpu_custom_call", output_to_operand_aliasing={{2}: (2, {})} | custom-call | bytes 240000000 | tf_op jit(solution)/shard_map/closing/pallas_call | solution.py:732
  1266.4 30.7 %sum_spread.1 = f32[64,128]{1,0:T(8,128)} custom-call(f32[32,64,128]{2,1,0:T(8,128)} %concatenate.69.part), custom_call_target="tpu_custom_call" | custom-call | bytes 60000000 | tf_op jit(solution)/shard_map/sum_spread/pallas_call | solution.py:907
  (450 shorter events, 205.6 us)
Async XLA Ops:
  7.2 108.5 %all-gather.7.cloned.1.call-start = ((), (), s32[]{:S(2)}) async-start(), calls=%async_computation.4 | async-start | bytes 7077888 | tf_op jit(solution)/shard_map/all_gather | solution.py:1496
  11.1 187.2 %all-gather.15.cloned.1.call-start = ((), (), s32[]{:S(2)}) async-start(), calls=%async_computation.12 | async-start | bytes 8650752 | tf_op jit(solution)/shard_map/all_gather | solution.py:1382
  103.8 246.0 %all-gather.9.cloned.1.call-start = ((), (), s32[]{:S(2)}) async-start(), calls=%async_computation.5 | async-start | bytes 17301504 | tf_op jit(solution)/shard_map/all_gather | solution.py:1375
  104.6 386.8 %all-gather.13.cloned.1.call-start = ((), (), s32[]{:S(2)}) async-start(), calls=%async_computation.7 | async-start | bytes 17301504 | tf_op jit(solution)/shard_map/all_gather | solution.py:1375
  109.6 31.0 %copy-start.76 = (f32[128,4]{0,1:T(4,128)}, f32[128,4]{0,1:T(4,128)S(1)}, u32[]{:S(2)}) copy-start(f32[128,4]{0,1:T(4,128)S(1)} %copy.142) | copy-start | bytes 6148
  109.6 28.8 %copy-start.79 = (f32[128,4]{0,1:T(4,128)}, f32[128,4]{0,1:T(4,128)S(1)}, u32[]{:S(2)}) copy-start(f32[128,4]{0,1:T(4,128)S(1)} %copy.141) | copy-start | bytes 6148
  121.1 19.4 %copy-start.9 = (f32[1024,512]{0,1:T(8,128)}, f32[1024,512]{0,1:T(8,128)S(1)}, u32[]{:S(2)}) copy-start(f32[1024,512]{0,1:T(8,128)S(1)} %get-tuple-element.316) | copy-start | bytes 6291460
  149.0 15.9 %copy-start.46 = (bf16[1024,512]{0,1:T(8,128)(2,1)}, bf16[1024,512]{0,1:T(8,128)(2,1)S(1)}, u32[]{:S(2)}) copy-start(bf16[1024,512]{0,1:T(8,128)(2,1)S(1)} %fusion.46) | copy-start | bytes 3145732
  197.8 368.2 %all-gather.11.cloned.1.call-start = ((), (), s32[]{:S(2)}) async-start(), calls=%async_computation.6 | async-start | bytes 17301504 | tf_op jit(solution)/shard_map/all_gather | solution.py:1375
  209.1 576.0 %reduce-scatter.5.cloned.1.call-start = ((), (), s32[]{:S(2)}) async-start(), calls=%async_computation.8 | async-start | bytes 18874368 | tf_op jit(solution)/shard_map/reduce_scatter | solution.py:1555
  230.2 119.5 %copy-start.90 = (s32[53]{0:T(128)}, s32[53]{0:T(128)S(1)}, u32[]{:S(2)}) copy-start(s32[53]{0:T(128)S(1)} %broadcast_add_fusion.4.refs_0_.refs_1_) | copy-start | bytes 640
  230.6 388.7 %copy-start.89 = (s32[53]{0:T(128)}, s32[53]{0:T(128)S(1)}, u32[]{:S(2)}) copy-start(s32[53]{0:T(128)S(1)} %broadcast_add_fusion.5.refs_0_.refs_1_) | copy-start | bytes 640
  231.3 118.5 %copy-start.92 = (s32[53]{0:T(128)}, s32[53]{0:T(128)S(1)}, u32[]{:S(2)}) copy-start(s32[53]{0:T(128)S(1)} %get-tuple-element.245.refs_1_.refs_2_) | copy-start | bytes 640
  232.6 117.1 %copy-start.97 = (s32[56]{0:T(128)}, s32[56]{0:T(128)S(1)}, u32[]{:S(2)}) copy-start(s32[56]{0:T(128)S(1)} %broadcast_add_fusion.2.refs_1_) | copy-start | bytes 676
  232.7 117.1 %copy-start.96 = (s32[56]{0:T(128)}, s32[56]{0:T(128)S(1)}, u32[]{:S(2)}) copy-start(s32[56]{0:T(128)S(1)} %broadcast_add_fusion.3.refs_1_) | copy-start | bytes 676
  234.3 115.5 %copy-start.59 = (s32[16,256,8]{1,2,0:T(8,128)}, s32[16,256,8]{1,2,0:T(8,128)S(1)}, u32[]{:S(2)}) copy-start(s32[16,256,8]{1,2,0:T(8,128)S(1)} %fusion.59) | copy-start | bytes 393220
  619.3 237.4 %reduce-scatter.7.cloned.1.call-start = ((), (), s32[]{:S(2)}) async-start(), calls=%async_computation.9 | async-start | bytes 18874368 | tf_op jit(solution)/shard_map/reduce_scatter | solution.py:1567
  668.5 456.0 %reduce-scatter.9.cloned.1.call-start = ((), (), s32[]{:S(2)}) async-start(), calls=%async_computation.10 | async-start | bytes 18874368 | tf_op jit(solution)/shard_map/reduce_scatter | solution.py:1411
  966.8 338.9 %reduce-scatter.11.cloned.1.call-start = ((), (), s32[]{:S(2)}) async-start(), calls=%async_computation.11 | async-start | bytes 2621440 | tf_op jit(solution)/shard_map/reduce_scatter | solution.py:1412
  1071.0 17.8 %copy-start.8 = (bf16[256,2048]{1,0:T(8,128)(2,1)S(1)}, bf16[256,2048]{1,0:T(8,128)(2,1)}, u32[]{:S(2)}) copy-start(bf16[256,2048]{1,0:T(8,128)(2,1)} %copy-done.7) | copy-start | bytes 3145732
  1071.0 17.8 %copy-start.41 = (bf16[4,256,512]{2,1,0:T(8,128)(2,1)S(1)}, bf16[4,256,512]{2,1,0:T(8,128)(2,1)}, u32[]{:S(2)}) copy-start(bf16[4,256,512]{2,1,0:T(8,128)(2,1)} %get-tuple-element.102) | copy-start | bytes 3145732
  1101.7 11.1 slice-start
  1101.7 11.1 slice-start.1
  1144.4 111.1 %copy-start.88 = (f32[256]{0:T(256)S(1)}, f32[256]{0:T(256)}, u32[]{:S(2)}) copy-start(f32[256]{0:T(256)} %get-tuple-element.308) | copy-start | bytes 3076
  (92 other events, 294.5 us)
Sparse Core Ops, SparseCore 0:
  11.2 53.0 all-gather.6
  103.9 74.8 all-gather.14
  181.8 150.5 all-gather.8
  335.3 114.1 all-gather.12
  452.8 113.0 all-gather.10
  619.4 117.6 reduce-scatter.4
  740.6 115.9 reduce-scatter.6
  966.9 130.2 reduce-scatter.8
  1124.6 57.1 reduce-scatter.10
where the time goes:
time: 1320 us
  Pallas kernels  918 us (70%)
  matrix products  92.7 us (7%)
  waiting for transfers between devices  92.1 us (7%)
  local copies, waits for them, and re-layouts  91.6 us (7%)
  other arithmetic  74.8 us (6%)
  blocking collectives  27.1 us (2%)
  between operations  18.1 us (1%)
    pallas_call x2, Pallas kernels, experts(): pl.pallas_call(functools.partial(while_used, expert_step), grid_spec=pltp...  206 us
    pallas_call x1, Pallas kernels, box_gather(): pl.pallas_call(functools.partial(box_gather_kernel, n), out_shape=jax.Sha...  113 us
    pallas_call x1, Pallas kernels, closing(): pl.pallas_call(functools.partial(closing_kernel, n), out_shape=[jax.Shape...  111 us
    pallas_call x2, Pallas kernels, combine(): pl.pallas_call(functools.partial(while_used, combine_step), grid_spec=plt...  108 us
    pallas_call x1, Pallas kernels, box_sum(): pl.pallas_call(functools.partial(box_sum_kernel, n, len(later)), out_shap...  105 us
    pallas_call x2, Pallas kernels, dispatch(): pl.pallas_call(functools.partial(while_used, dispatch_step), grid_spec=pl...  93.8 us
    pallas_call x1, Pallas kernels, chain_gather(): pl.pallas_call(functools.partial(chain_gather_kernel, n, pieces, len(late...  89.4 us
    all_gather x3, waiting for transfers between devices, gather_slowly(): return lax.all_gather(own, ('dp', 'tensor'), axis=0, tiled=True)  74.6 us
  transfers between devices with their start and end apart: 9, of which 2 were waited for; matrix products, arithmetic and copies ran while one was open for 17% of the time, Pallas kernels for 58%

commit v1 on v0

--- a/solution.py
+++ b/solution.py
@@ -388,17 +388,23 @@
     return me, {bit: {"dp": flip(me, bit)} for bit in (1, 2, 4)}
 
 
-def box_gather_kernel(n, own, out, local_sem, z_send, z_recv, near_send, near_recv, on_send, on_recv, side_send, side_recv):
+def box_gather_kernel(n, own, first, second, local_sem, z_send, z_recv, near_send, near_recv, on_send, on_recv, side_send, side_recv):
     spot, sides = both_ways(n)
     me, near = box_devices()
     half = own.shape[0] // 2
     greet([near[1], near[2], near[4]], sides)
-    keep = pltpu.make_async_copy(own, out.at[me, spot], local_sem)
-    keep.start()
+    keep = [
+        pltpu.make_async_copy(
+            own.at[pl.ds(part * half, half)], (first, second)[part].at[me, spot], local_sem.at[part]
+        )
+        for part in (0, 1)
+    ]
+    for one in keep:
+        one.start()
     sends = []
 
     def piece(seq, shard, part):
-        return out.at[seq, shard, pl.ds(part * half, half)]
+        return (first, second)[part].at[seq, shard]
 
     def start(condition, one):
         sends.append((condition, one))
@@ -461,7 +467,8 @@
                     if bit & one:
                         seq = flip(seq, one)
                 await_piece(spot >= 0, piece(seq, shard, part), side_recv.at[slot, shard, part])
-    keep.wait()
+    for one in keep:
+        one.wait()
     for condition, one in sends:
 
         @pl.when(condition)
@@ -475,19 +482,19 @@
     sem = pltpu.SemaphoreType.DMA
     out = pl.pallas_call(
         functools.partial(box_gather_kernel, n),
-        out_shape=jax.ShapeDtypeStruct((8, n, rows, width), own.dtype),
+        out_shape=[jax.ShapeDtypeStruct((8, n, rows // 2, width), own.dtype)] * 2,
         in_specs=[pl.BlockSpec(memory_space=pl.ANY)],
-        out_specs=pl.BlockSpec(memory_space=pl.ANY),
-        scratch_shapes=[sem]
+        out_specs=[pl.BlockSpec(memory_space=pl.ANY)] * 2,
+        scratch_shapes=[sem((2,))]
         + [sem((2, n - 1, 2))] * 2
         + [sem((2, n, 2))] * 2
         + [sem((2, n))] * 2
         + [sem((4, n, 2))] * 2,
         compiler_params=pltpu.CompilerParams(collective_id=3, has_side_effects=True),
-        cost_estimate=transfer(75),
+        cost_estimate=transfer(140),
         name="box_gather",
     )(own)
-    return out.reshape(8 * n * rows, width)
+    return [half.reshape(4 * n * rows, width) for half in out]
 
 
 def order_of(spot, n):
@@ -1362,18 +1369,19 @@
     )
 
 
-def gather_all(own):
+def gather_halves(own):
     if lax.axis_size("dp") == 8:
         return box_gather(own)
-    return lax.all_gather(
-        lax.all_gather(own, "tensor", axis=0, tiled=True), "dp", axis=0, tiled=True
-    )
+    few = own.shape[0] // 2
+    return [gather_slowly(own[:few]), gather_slowly(own[few:])]
 
 
 def gather_slowly(own):
     if lax.axis_size("dp") == 8:
         return lax.all_gather(own, ("dp", "tensor"), axis=0, tiled=True)
-    return gather_all(own)
+    return lax.all_gather(
+        lax.all_gather(own, "tensor", axis=0, tiled=True), "dp", axis=0, tiled=True
+    )
 
 
 def gather_output(own):
@@ -1513,9 +1521,9 @@
     plan = Plan(mesh_dp * n * few, n * few, gate_proj.shape[0])
     base = (lax.axis_index("dp") * plan.local).astype(jnp.int32)
     all_routes = all_routes.reshape(mesh_dp, n, 2, few, TOP)
-    route = [
-        routing(plan, all_routes[:, :, index].reshape(-1, TOP), base) for index in range(2)
-    ]
+    both = jnp.moveaxis(all_routes, 2, 0).reshape(2, -1, TOP)
+    both = jax.vmap(lambda routes: routing(plan, routes, base))(both)
+    route = [{name: value[index] for name, value in both.items()} for index in range(2)]
     all_grad = [gather_slowly(later)]
     query = jnp.dot(group_normed, w_query, preferred_element_type=jnp.float32)
     keys = jnp.dot(group_normed, w_key, preferred_element_type=jnp.float32)
@@ -1540,7 +1548,7 @@
     middle = residual + attn_local
     inv_post = lax.rsqrt(jnp.mean(middle * middle, -1, keepdims=True) + epsilon)
     post_normed = (middle * inv_post * post_gain).astype(jnp.bfloat16)
-    all_post = [gather_all(post_normed[:few]), gather_slowly(post_normed[few:])]
+    all_post = gather_halves(post_normed)
     grads, outs, backs, router_parts = [], [], [], []
     for index in range(2):
         rows, portion, *outs = dispatch(
@@ -1550,14 +1558,14 @@
             plan, route[index], base, rows, gate_proj, up_proj, down_proj, grads
         )
         if index == 0:
-            later = [all_post[1], all_grad[1]]
+            later = [all_grad[1]]
         else:
             later = [lax.psum_scatter(backs[0], "dp", scatter_dimension=0, tiled=True)]
         out, back, router_part, *later = combine(
             plan, route[index], results, portion, all_post[index], router_full, later
         )
         if index == 0:
-            all_post[1], all_grad[1] = later
+            all_grad[1] = later[0]
         else:
             early = later[0]
         outs.append(out)
@@ -1565,13 +1573,9 @@
         router_parts.append(router_part)
     gate_weight_grad, up_weight_grad, down_weight_grad = grads
     first_out = lax.psum_scatter(outs[0], "dp", scatter_dimension=0, tiled=True)
-    early = jnp.concatenate(
-        [early.reshape(n, few, D), first_out.reshape(n, few, D)], 1
-    ).reshape(-1, D)
     late, early, outs = sum_all(backs[1], early, outs[1:])
-    early, first_out = early[:few], early[few:].astype(jnp.bfloat16)
     grad_post = jnp.concatenate([early, late], 0)
-    moe_local = jnp.concatenate([first_out, sum_slowly(outs[0])], 0)
+    second_out = lax.psum_scatter(outs[0], "dp", scatter_dimension=0, tiled=True)
     router_part = router_parts[0] + router_parts[1]
     router_part = router_part.T
     post_gain_part = jnp.sum(grad_post * middle * inv_post, 0)
@@ -1579,10 +1583,18 @@
         grad_post, middle, inv_post, post_gain, D
     )
     change = grad_middle.astype(jnp.bfloat16)
-    grad_mixed, _ = swap(
+    grad_mixed, first_out = swap(
         jnp.stack([nn_dot(change, w_output[index]).astype(jnp.bfloat16) for index in range(n)]),
-        jnp.zeros((16, 128), jnp.bfloat16),
+        first_out,
         2,
+    )
+    moe_local = lax.psum_scatter(
+        jnp.concatenate(
+            [first_out.reshape(n, few, D), second_out.reshape(n, few, D)], 1
+        ).reshape(-1, D),
+        "tensor",
+        scatter_dimension=0,
+        tiled=True,
     )
     output_parts = [tn_dot(change, mixed_own[index]).astype(jnp.bfloat16) for index in range(n)]
     grad_query_rot, grad_key_rot, grad_value_heads = attend_backward(
@@ -1652,30 +1664,26 @@
         jnp.where(mine, gains, 0.0),
         ((0, 0), (0, 0), (0, max(router.shape[0] - HD // mesh_dp, 0)), (0, 0)),
     ).reshape(D, 2 * heads)
-    small = jnp.concatenate(
-        [
-            router_part,
-            pre_gain_part[:, None],
-            post_gain_part[:, None],
-            gains,
-            jnp.zeros((D, 128 - E - 2 - 2 * heads), jnp.float32),
-        ],
-        1,
-    )
-    small = sum_spread(small.reshape(-1, router.shape[0], 128))
-    gain_grads = small[: HD // mesh_dp, E + 2 : E + 2 + 2 * heads]
+    own = router.shape[0]
+    block = jnp.concatenate(
+        [router_part, gains, jnp.zeros((D, 128 - E - 2 * heads), jnp.float32)], 1
+    )
+    block = jnp.pad(block.reshape(-1, own, 128), ((0, 0), (0, 8), (0, 0)))
+    block = block.at[:, own, :own].set(post_gain_part.reshape(-1, own))
+    small = sum_spread(block.at[:, own + 1, :own].set(pre_gain_part.reshape(-1, own)))
+    gain_grads = small[: HD // mesh_dp, E : E + 2 * heads]
     return (
         layer_out,
         input_grad,
-        small[:, E],
+        small[own + 1, :own],
         gain_grads[:, :heads],
         gain_grads[:, heads : 2 * heads],
         weight_sums[1],
         weight_sums[2],
         weight_sums[3],
         weight_sums[0],
-        small[:, E + 1],
-        small[:, :E],
+        small[own, :own],
+        small[:own, :E],
         gate_weight_grad,
         up_weight_grad,
         down_weight_grad,

time: 1320 us -> 1330 us (level)
  Pallas kernels: 918 us -> 998 us
  waiting for transfers between devices: 92.1 us -> 28.7 us
    pallas_call x1, Pallas kernels: 113 us -> 210 us  [box_gather(): pl.pallas_call(functools.partial(box_gather_kernel, n), out_shape=[jax.Sh...]
    all_gather x3 -> x2, waiting for transfers between devices: 74.6 us -> 0.04 us  [gather_slowly(): return lax.all_gather(own, ('dp', 'tensor'), axis=0, tiled=True)]
    reduce_scatter x2, waiting for transfers between devices: 0.01 us -> 27.8 us  [the longest x1 27.8 us: body(): lax.psum_scatter(outs[0], 'dp', scatter_dimension=0, tiled=True)]
    reduce_scatter x1, waiting for transfers between devices: 16.6 us -> 0.01 us  [body(): first_out = lax.psum_scatter(outs[0], 'dp', scatter_dimension=0, tiled=True)]
    pallas_call x2, Pallas kernels: 60.8 us -> 47.3 us  [swap(): pl.pallas_call(functools.partial(swap_kernel, n), out_shape=[jax.ShapeDty...]
    unnamed x227 -> x205, local copies, waits for them, and re-layouts: 35.9 us -> 39.8 us
  transfers between devices with their start and end apart: 9 -> 8, of which waited for: 2 -> 1; matrix products, arithmetic and copies ran while one was open for 17% -> 16% of each run, Pallas kernels for 58% -> 72%
where the time goes in v1:
time: 1330 us; the launch traced here: 1320 us
  Pallas kernels  998 us (75%)
  matrix products  94.1 us (7%)
  local copies, waits for them, and re-layouts  85.5 us (6%)
  other arithmetic  68.1 us (5%)
  waiting for transfers between devices  28.7 us (2%)
  blocking collectives  24 us (2%)
  between operations  16 us (1%)
    pallas_call x1, Pallas kernels, box_gather(): pl.pallas_call(functools.partial(box_gather_kernel, n), out_shape=[jax.Sh...  210 us
    pallas_call x2, Pallas kernels, experts(): pl.pallas_call(functools.partial(while_used, expert_step), grid_spec=pltp...  204 us
    pallas_call x1, Pallas kernels, box_sum(): pl.pallas_call(functools.partial(box_sum_kernel, n, len(later)), out_shap...  110 us
    pallas_call x2, Pallas kernels, combine(): pl.pallas_call(functools.partial(while_used, combine_step), grid_spec=plt...  108 us
    pallas_call x1, Pallas kernels, closing(): pl.pallas_call(functools.partial(closing_kernel, n), out_shape=[jax.Shape...  104 us
    pallas_call x2, Pallas kernels, dispatch(): pl.pallas_call(functools.partial(while_used, dispatch_step), grid_spec=pl...  94 us
    pallas_call x1, Pallas kernels, chain_gather(): pl.pallas_call(functools.partial(chain_gather_kernel, n, pieces, len(late...  89.4 us
    pallas_call x2, Pallas kernels, swap(): pl.pallas_call(functools.partial(swap_kernel, n), out_shape=[jax.ShapeDty...  47.3 us
  transfers between devices with their start and end apart: 8, of which 1 were waited for; matrix products, arithmetic and copies ran while one was open for 16% of the time, Pallas kernels for 72%

profile of v1, /device:TPU:0, one launch (start us, length us, event | category | flops | bytes accessed | tf_op | source)
XLA Modules:
  0.0 1315.8 jit_solution(6675656050326484109)
XLA Ops:
  14.4 89.4 %chain_gather.1 = (bf16[4,256,2048]{2,1,0:T(8,128)(2,1)}, bf16[128,2048]{1,0:T(8,128)(2,1)}, bf16[256,512]{1,0:T(8,128)(2,1)}, bf16[32,80,128]{2,1,0:T(8,128)(2,1)}) custom-call(bf16[256,2048]{1,0:T(8,128)(2,1)} %bitcast.312, bf16[128,2048]{1,0:T(8,128)(2,1)} %get-tuple-element.278.refs_0_, ...), custom_call_target="tpu_custom_call", output_to_operand_aliasing={{1}: (1, {}), {2}: (2, {})} | custom-call | bytes 195000000 | tf_op jit(solution)/shard_map/chain_gather/pallas_call | solution.py:240
  121.1 6.2 multiply_reduce_fusion.6
  127.3 10.6 all-reduce.6
  149.1 7.8 fusion.115
  156.8 8.1 fusion
  164.9 7.8 fusion.52
  175.4 22.6 %swap.2 = (bf16[4,256,512]{2,1,0:T(8,128)(2,1)}, bf16[128,2048]{1,0:T(8,128)(2,1)}) custom-call(bf16[4,256,512]{2,1,0:T(8,128)(2,1)} %copy.157.part, bf16[128,2048]{1,0:T(8,128)(2,1)} %get-tuple-element.277._later), custom_call_target="tpu_custom_call", output_to_operand_aliasing={{1}: (1, {})} | custom-call | bytes 75000000 | tf_op jit(solution)/shard_map/swap/pallas_call | solution.py:790
  230.1 210.2 %box_gather.1 = (bf16[8,4,128,2048]{3,2,1,0:T(8,128)(2,1)}, bf16[8,4,128,2048]{3,2,1,0:T(8,128)(2,1)}) custom-call(bf16[256,2048]{1,0:T(8,128)(2,1)} %multiply_convert_fusion.2.own), custom_call_target="tpu_custom_call" | custom-call | bytes 420000000 | tf_op jit(solution)/shard_map/box_gather/pallas_call | solution.py:483
  440.4 46.5 %dispatch.2 = (bf16[20352,4224]{1,0:T(8,128)(2,1)}, bf16[4096,128]{1,0:T(8,128)(2,1)}) custom-call(s32[1]{0:T(128)} %get-tuple-element.333.used, s32[53]{0:T(128)} %get-tuple-element.328.refs_0_.refs_1_, s32[53]{0:T(128)} %get-tuple-element.353.refs_1_.refs_2_, bf16[4096,2048]{1,0:T(8,128)(2,1)} %bitcast.310, ...), custom_call_target="tpu_custom_call" | custom-call | bytes 135000000 | tf_op jit(solution)/shard_map/dispatch/pallas_call | solution.py:1082
  486.9 94.6 %experts.2 = (bf16[14336,4224]{1,0:T(8,128)(2,1)}, f32[8,2048,256]{2,1,0:T(8,128)}, f32[8,2048,256]{2,1,0:T(8,128)}, f32[8,2048,256]{2,1,0:T(8,128)}) custom-call(s32[1]{0:T(128)} %get-tuple-element.331.used, s32[896]{0:T(1024)} %reshape.719.refs_0_, s32[56]{0:T(128)} %get-tuple-element.322.refs_1_, s32[56]{0:T(128)} %get-tuple-element.355.refs_2_, ...), custom_call_target="tpu_custom_call" | custom-call | bytes 240000000 | tf_op jit(solution)/shard_map/experts/pallas_call | solution.py:1225
  581.5 53.6 %combine.2 = (bf16[4096,2048]{1,0:T(8,128)(2,1)}, bf16[4096,2048]{1,0:T(8,128)(2,1)}, f32[64,2048]{1,0:T(8,128)}, bf16[4096,2048]{1,0:T(8,128)(2,1)}) custom-call(s32[1]{0:T(128)} %get-tuple-element.333.used, s32[1272]{0:T(1024)} %squeeze.142.refs_0_, s32[53]{0:T(128)} %get-tuple-element.328.refs_0_.refs_1_, ...), custom_call_target="tpu_custom_call", output_to_operand_aliasing={{3}: (10, {})} | custom-call | bytes 150000000 | tf_op jit(solution)/shard_map/combine/pallas_call | solution.py:1322
  635.4 47.6 %dispatch.3 = (bf16[20352,4224]{1,0:T(8,128)(2,1)}, bf16[4096,128]{1,0:T(8,128)(2,1)}, bf16[4096,2048]{1,0:T(8,128)(2,1)}) custom-call(s32[1]{0:T(128)} %get-tuple-element.334.used, s32[53]{0:T(128)} %get-tuple-element.329.refs_0_.refs_1_, s32[53]{0:T(128)} %get-tuple-element.352.refs_1_.refs_2_, ...), custom_call_target="tpu_custom_call", output_to_operand_aliasing={{2}: (7, {})} | custom-call | bytes 135000000 | tf_op jit(solution)/shard_map/dispatch/pallas_call | solution.py:1082
  687.0 109.1 %experts.3 = (bf16[14336,4224]{1,0:T(8,128)(2,1)}, f32[8,2048,256]{2,1,0:T(8,128)}, f32[8,2048,256]{2,1,0:T(8,128)}, f32[8,2048,256]{2,1,0:T(8,128)}) custom-call(s32[1]{0:T(128)} %get-tuple-element.332.used, s32[896]{0:T(1024)} %reshape.717.refs_0_, s32[56]{0:T(128)} %get-tuple-element.323.refs_1_, ...), custom_call_target="tpu_custom_call", output_to_operand_aliasing={{1}: (11, {}), {2}: (12, {}), {3}: (13, {})} | custom-call | bytes 240000000 | tf_op jit(solution)/shard_map/experts/pallas_call | solution.py:1225
  796.2 54.1 %combine.3 = (bf16[4096,2048]{1,0:T(8,128)(2,1)}, bf16[4096,2048]{1,0:T(8,128)(2,1)}, f32[64,2048]{1,0:T(8,128)}, bf16[512,2048]{1,0:T(8,128)(2,1)}) custom-call(s32[1]{0:T(128)} %get-tuple-element.334.used, s32[1272]{0:T(1024)} %squeeze.134.refs_0_, s32[53]{0:T(128)} %get-tuple-element.329.refs_0_.refs_1_, ...), custom_call_target="tpu_custom_call", output_to_operand_aliasing={{3}: (10, {})} | custom-call | bytes 150000000 | tf_op jit(solution)/shard_map/combine/pallas_call | solution.py:1322
  850.3 110.0 %box_sum.1 = (f32[128,2048]{1,0:T(8,128)}, f32[128,2048]{1,0:T(8,128)}, bf16[4096,2048]{1,0:T(8,128)(2,1)}) custom-call(bf16[8,4,128,2048]{3,2,1,0:T(8,128)(2,1)} %bitcast.317, bf16[4,128,2048]{2,1,0:T(8,128)(2,1)} %bitcast.325, bf16[4096,2048]{1,0:T(8,128)(2,1)} %get-tuple-element.148.refs_0_), custom_call_target="tpu_custom_call", output_to_operand_aliasing={{2}: (2, {})} | custom-call | bytes 270000000 | tf_op jit(solution)/shard_map/box_sum/pallas_call | solution.py:817
  983.1 24.7 %swap.3 = (bf16[4,256,512]{2,1,0:T(8,128)(2,1)}, bf16[512,2048]{1,0:T(8,128)(2,1)}) custom-call(bf16[4,256,512]{2,1,0:T(8,128)(2,1)} %pad_maximum_fusion.1.part, bf16[512,2048]{1,0:T(8,128)(2,1)} %reduce-scatter.7.cloned.1.call-done._later), custom_call_target="tpu_custom_call", output_to_operand_aliasing={{1}: (1, {})} | custom-call | bytes 75000000 | tf_op jit(solution)/shard_map/swap/pallas_call | solution.py:790
  1010.7 11.0 multiply_reduce_fusion
  1021.7 8.7 multiply_convert_fusion
  1034.1 6.6 bitcast_multiply_fusion.4
  1056.6 27.8 %reduce-scatter.9.cloned.1.call-done = bf16[512,2048]{1,0:T(8,128)(2,1)} async-done(((bf16[4096,2048]{1,0:T(8,128)(2,1)}), bf16[512,2048]{1,0:T(8,128)(2,1)}) %reduce-scatter.9.cloned.1.call-update) | async-done | bytes 2097168 | tf_op jit(solution)/shard_map/reduce_scatter | solution.py:1578
  1094.2 13.5 %all-reduce.5 = (f32[1024]{0:T(1024)S(1)}, f32[1024]{0:T(1024)}) all-reduce(f32[1024]{0:T(1024)S(1)} %get-tuple-element.222, f32[1024]{0:T(1024)S(1)} %get-tuple-element.224), channel_id=1, replica_groups=mesh['dp'=8,'tensor'=4] {'tensor'}, use_global_device_ids=true, to_apply=%region_34.35 | all-reduce | flops 2048 | bytes 16384 | tf_op jit(solution)/shard_map/psum | solution.py:39
  1148.4 6.0 add_convert_fusion
  1154.4 104.0 %closing.1 = (f32[256,2048]{1,0:T(8,128)}, f32[4,256,512]{2,1,0:T(8,128)}, f32[256,2048]{1,0:T(8,128)}) custom-call(bf16[4,256,2048]{2,1,0:T(8,128)(2,1)} %bitcast.319, bf16[7,8,256,512]{3,2,1,0:T(8,128)(2,1)} %constant_dynamic-update-slice_fusion.2.part, f32[256,2048]{1,0:T(8,128)} %copy-done.1), custom_call_target="tpu_custom_call", output_to_operand_aliasing={{2}: (2, {})} | custom-call | bytes 240000000 | tf_op jit(solution)/shard_map/closing/pallas_call | solution.py:739
  1264.5 32.0 %sum_spread.1 = f32[72,128]{1,0:T(8,128)} custom-call(f32[32,72,128]{2,1,0:T(8,128)} %scatter.9.part), custom_call_target="tpu_custom_call" | custom-call | bytes 60000000 | tf_op jit(solution)/shard_map/sum_spread/pallas_call | solution.py:914
  (396 shorter events, 187.4 us)
Async XLA Ops:
  7.2 6.1 copy-start.40
  7.2 108.5 %all-gather.6.cloned.1.call-start = ((), (), s32[]{:S(2)}) async-start(), calls=%async_computation.4 | async-start | bytes 7077888 | tf_op jit(solution)/shard_map/all_gather | solution.py:1504
  11.1 207.6 %all-gather.12.cloned.1.call-start = ((), (), s32[]{:S(2)}) async-start(), calls=%async_computation.11 | async-start | bytes 8650752 | tf_op jit(solution)/shard_map/all_gather | solution.py:1390
  103.8 336.6 %all-gather.8.cloned.1.call-start = ((), (), s32[]{:S(2)}) async-start(), calls=%async_computation.5 | async-start | bytes 17301504 | tf_op jit(solution)/shard_map/all_gather | solution.py:1381
  104.5 476.9 %all-gather.10.cloned.1.call-start = ((), (), s32[]{:S(2)}) async-start(), calls=%async_computation.6 | async-start | bytes 17301504 | tf_op jit(solution)/shard_map/all_gather | solution.py:1381
  109.5 31.1 %copy-start.69 = (f32[128,4]{0,1:T(4,128)}, f32[128,4]{0,1:T(4,128)S(1)}, u32[]{:S(2)}) copy-start(f32[128,4]{0,1:T(4,128)S(1)} %copy.126) | copy-start | bytes 6148
  109.6 28.9 %copy-start.72 = (f32[128,4]{0,1:T(4,128)}, f32[128,4]{0,1:T(4,128)S(1)}, u32[]{:S(2)}) copy-start(f32[128,4]{0,1:T(4,128)S(1)} %copy.125) | copy-start | bytes 6148
  121.1 19.5 %copy-start.9 = (f32[1024,512]{0,1:T(8,128)}, f32[1024,512]{0,1:T(8,128)S(1)}, u32[]{:S(2)}) copy-start(f32[1024,512]{0,1:T(8,128)S(1)} %get-tuple-element.336) | copy-start | bytes 6291460
  149.0 15.9 %copy-start.43 = (bf16[1024,512]{0,1:T(8,128)(2,1)}, bf16[1024,512]{0,1:T(8,128)(2,1)S(1)}, u32[]{:S(2)}) copy-start(bf16[1024,512]{0,1:T(8,128)(2,1)S(1)} %fusion.46) | copy-start | bytes 3145732
  156.8 8.1 copy-start.58
  164.9 7.9 copy-start.67
  173.6 24.8 %copy-start.33 = (bf16[32,80,128]{2,1,0:T(8,128)(2,1)S(1)}, bf16[32,80,128]{2,1,0:T(8,128)(2,1)}, u32[]{:S(2)}) copy-start(bf16[32,80,128]{2,1,0:T(8,128)(2,1)} %get-tuple-element.127) | copy-start | bytes 1966084
  198.0 598.2 %reduce-scatter.5.cloned.1.call-start = ((), (), s32[]{:S(2)}) async-start(), calls=%async_computation.7 | async-start | bytes 18874368 | tf_op jit(solution)/shard_map/reduce_scatter | solution.py:1563
  207.3 20.8 %copy-start.60 = (f32[2048]{0:T(1024)}, f32[2048]{0:T(1024)S(1)}, u32[]{:S(2)}) copy-start(f32[2048]{0:T(1024)S(1)} %reshape.742) | copy-start | bytes 24580
  228.2 212.2 %copy-start.80 = (f32[256]{0:T(256)}, f32[256]{0:T(256)S(1)}, u32[]{:S(2)}) copy-start(f32[256]{0:T(256)S(1)} %get-tuple-element.315) | copy-start | bytes 3076
  635.1 348.0 %reduce-scatter.7.cloned.1.call-start = ((), (), s32[]{:S(2)}) async-start(), calls=%async_computation.8 | async-start | bytes 18874368 | tf_op jit(solution)/shard_map/reduce_scatter | solution.py:1575
  683.0 401.5 %reduce-scatter.9.cloned.1.call-start = ((), (), s32[]{:S(2)}) async-start(), calls=%async_computation.9 | async-start | bytes 18874368 | tf_op jit(solution)/shard_map/reduce_scatter | solution.py:1578
  960.4 345.6 %reduce-scatter.11.cloned.1.call-start = ((), (), s32[]{:S(2)}) async-start(), calls=%async_computation.10 | async-start | bytes 5242880 | tf_op jit(solution)/shard_map/reduce_scatter | solution.py:1591
  962.4 5.9 copy-start.54
  1021.7 8.7 copy-start.21
  1117.7 10.4 slice-start
  1117.7 10.4 slice-start.1
  1154.4 104.0 %copy-start.82 = (f32[256]{0:T(256)S(1)}, f32[256]{0:T(256)}, u32[]{:S(2)}) copy-start(f32[256]{0:T(256)} %get-tuple-element.313) | copy-start | bytes 3076
  1258.5 42.8 %copy-start.48 = (f32[4,256,512]{2,1,0:T(8,128)S(1)}, f32[4,256,512]{2,1,0:T(8,128)}, u32[]{:S(2)}) copy-start(f32[4,256,512]{2,1,0:T(8,128)} %get-tuple-element.159) | copy-start | bytes 6291460
  (80 other events, 224.3 us)
Sparse Core Ops, SparseCore 0:
  11.2 53.0 all-gather.5
  103.9 74.7 all-gather.11
  181.8 157.4 all-gather.7
  342.1 136.9 all-gather.9
  635.2 126.1 reduce-scatter.4
  764.8 124.1 reduce-scatter.6
  960.5 123.9 reduce-scatter.8
  1089.4 82.9 reduce-scatter.10
